TPU v7x, 128 devices: a whole 4x4x4 slice. The times are simulated.
128 devices in a mesh: ctx: 16 (over z, x), head: 8 (over y, core).
Axes of the slice: x: 4, y: 4, z: 4, core: 2. Of those that a mesh axis runs over, the one named last changes fastest.
Arguments:
- queries: bfloat16 [4096, 2048], P('ctx', 'head'), may hold values from -110 to 110
- keys: bfloat16 [65536, 128], P('ctx'), may hold values from -6 to 6
- values: bfloat16 [65536, 128], P('ctx'), may hold values from -6 to 6
- w_out: bfloat16 [2048, 16384], P(None, 'head'), may hold values from -0.125 to 0.125
- new_counts: int32 [8], replicated, may hold values from 1 to 2048, as said below
- prior_lengths: int32 [8], replicated, may hold values from 1 to 30720, as said below
Outputs:
- mixed: bfloat16 [4096, 16384], P('ctx', 'head')
Inputs may be any that keep to these rules, and one draw needn't show every extreme that they name: `new_counts`: every request has at least one new token; the counts add up to 4096. `prior_lengths`: every request has at least one cached token; the lengths add up to 61440.
All inputs are finite; a program needn't handle non-finite values.
Results may differ from a plain program's by a relative error of at most 0.011.
Values may be sent and summed in bfloat16 or wider, within the bound.
A program may use at most 384 MiB of HBM per device.

v0:
```python
import jax
import jax.numpy as jnp
from jax import lax
from jax.sharding import PartitionSpec as P

NEG = -1e30


def from_behind(value, axis, steps):
    count = lax.axis_size(axis)
    pairs = [(source, (source + steps) % count) for source in range(count)]
    return lax.ppermute(value, axis, pairs)


def row_info(index, ends, table):
    req = jnp.sum((index[:, None] >= ends[None, :]).astype(jnp.int32), axis=1)
    onehot = (req[:, None] == jnp.arange(ends.shape[0], dtype=jnp.int32)[None, :]).astype(jnp.int32)
    return (req, index + jnp.sum(onehot * table[None, :], axis=1))


def partial_block(q_block, q_req, q_pos, key_rows, value_rows, k_req, k_pos):
    count = q_block.shape[0]
    width = key_rows.shape[1]
    heads = q_block.shape[1] // width
    q_three = q_block.reshape(count, heads, width)
    scores = jnp.einsum(
        "nhd,kd->nhk", q_three, key_rows, preferred_element_type=jnp.float32
    ) * width ** (-0.5)
    allowed = ((q_req[:, None] == k_req[None, :]) & (k_pos[None, :] <= q_pos[:, None]))[:, None, :]
    scores = jnp.where(allowed, scores, NEG)
    top = jnp.max(scores, axis=2)
    weights = jnp.where(allowed, jnp.exp(scores - top[:, :, None]), 0.0)
    total = jnp.sum(weights, axis=2)
    summed = jnp.einsum(
        "nhk,kd->nhd", weights.astype(jnp.bfloat16), value_rows, preferred_element_type=jnp.float32
    )
    live = total > 0.0
    safe = jnp.where(live, total, 1.0)
    return (summed / safe[:, :, None], jnp.where(live, top + jnp.log(safe), NEG))


def merge_pair(out_one, lse_one, out_two, lse_two):
    top = jnp.maximum(lse_one, lse_two)
    left = jnp.exp(lse_one - top)
    right = jnp.exp(lse_two - top)
    total = left + right
    merged = (left[:, :, None] * out_one + right[:, :, None] * out_two) / total[:, :, None]
    return (merged, top + jnp.log(total))


def body(queries, keys, values, w_out, new_counts, prior_lengths):
    ctx_count = lax.axis_size("ctx")
    device = lax.axis_index("ctx")
    rows = queries.shape[0]
    cache = keys.shape[0]
    width = keys.shape[1]
    heads = queries.shape[1] // width
    q_ends = jnp.cumsum(new_counts)
    q_table = prior_lengths - (q_ends - new_counts)
    spans = new_counts + prior_lengths
    k_ends = jnp.cumsum(spans)
    k_table = spans - k_ends

    def query_info(block):
        return row_info(block * rows + jnp.arange(rows, dtype=jnp.int32), q_ends, q_table)

    empty_out = jnp.zeros((rows, heads, width), jnp.float32)
    empty_lse = jnp.full((rows, heads), NEG, jnp.float32)
    k_req, k_pos = row_info(device * cache + jnp.arange(cache, dtype=jnp.int32), k_ends, k_table)

    def step(turn, state):
        q_now, out, lse = state
        anchor = (device - turn) % ctx_count
        q_req, q_pos = query_info(anchor)
        part_out, part_lse = partial_block(q_now, q_req, q_pos, keys, values, k_req, k_pos)
        out, lse = merge_pair(out, lse, part_out, part_lse)
        q_now = from_behind(q_now, "ctx", 1)
        out, lse = from_behind((out, lse), "ctx", 1)
        return (q_now, out, lse)

    last = lax.fori_loop(0, ctx_count, step, (queries, empty_out, empty_lse))
    out = last[1]
    attended = out.reshape(rows, heads * width).astype(jnp.bfloat16)
    mixed = jnp.dot(
        lax.all_gather(attended, "head", axis=1, tiled=True),
        w_out,
        preferred_element_type=jnp.float32,
    )
    return mixed.astype(jnp.bfloat16)


def solution(mesh):
    return jax.shard_map(
        body,
        mesh=mesh,
        in_specs=(P("ctx", "head"), P("ctx", None), P("ctx", None), P(None, "head"), P(), P()),
        out_specs=P("ctx", "head"),
        check_vma=False,
    )
```

profile of v0, /device:TPU:7, one launch (start us, length us, event | category | flops | bytes accessed | tf_op | source)
XLA Modules:
  0.0 402.1 jit_solution(11989780486474361892)
XLA Ops:
  9.4 327.3 %while.19 = (s32[]{:T(128)}, bf16[256,256]{1,0:T(8,128)(2,1)S(1)}, f32[256,2,128]{2,0,1:T(8,128)S(1)}, f32[256,2]{0,1:T(2,128)S(1)}, s32[]{:T(128)}, /*index=5*/...) while((s32[]{:T(128)}, bf16[256,256]{1,0:T(8,128)(2,1)S(1)}, ...), condition=%wide.region_9.10_spmd, body=%wide.region_4.9_spmd.sunk | while | flops 1104494336 | bytes 38225396 | solution.py:81
  16.5 3.5 fusion.45
  24.1 6.0 %collective-permute-done.2 = f32[256,2]{0,1:T(2,128)S(1)} collective-permute-done((f32[256,2]{0,1:T(2,128)S(1)}, f32[256,2]{0,1:T(2,128)S(1)}, u32[]{:S(2)}, u32[]{:S(2)}) %collective-permute-start.2) | collective-permute-done | bytes 2080 | tf_op jit(solution)/shard_map/while/body/eval_jaxpr/ppermute | solution.py:12
  37.2 3.5 fusion.45
  40.7 3.7 collective-permute-start.1
  44.8 6.6 %collective-permute-done.2 = f32[256,2]{0,1:T(2,128)S(1)} collective-permute-done((f32[256,2]{0,1:T(2,128)S(1)}, f32[256,2]{0,1:T(2,128)S(1)}, u32[]{:S(2)}, u32[]{:S(2)}) %collective-permute-start.2) | collective-permute-done | bytes 2080 | tf_op jit(solution)/shard_map/while/body/eval_jaxpr/ppermute | solution.py:12
  62.0 4.4 %collective-permute-start.1 = (f32[256,2,128]{2,0,1:T(8,128)S(1)}, f32[256,2,128]{2,0,1:T(8,128)S(1)}, u32[]{:S(2)}, u32[]{:S(2)}) collective-permute-start(f32[256,2,128]{2,0,1:T(8,128)S(1)} %fusion.45), channel_id=1, source_target_pairs={{0,8},{8,16},{16,24},{24,32},{32,40},{40,48},{48,56},{56,64},{64,7... | collective-permute-start | bytes 786440 | tf_op jit(solution)/shard_map/while/body/eval_jaxpr/ppermute | solution.py:12
  66.5 5.8 %collective-permute-done.2 = f32[256,2]{0,1:T(2,128)S(1)} collective-permute-done((f32[256,2]{0,1:T(2,128)S(1)}, f32[256,2]{0,1:T(2,128)S(1)}, u32[]{:S(2)}, u32[]{:S(2)}) %collective-permute-start.2) | collective-permute-done | bytes 2080 | tf_op jit(solution)/shard_map/while/body/eval_jaxpr/ppermute | solution.py:12
  79.4 3.5 fusion.45
  82.9 4.4 %collective-permute-start.1 = (f32[256,2,128]{2,0,1:T(8,128)S(1)}, f32[256,2,128]{2,0,1:T(8,128)S(1)}, u32[]{:S(2)}, u32[]{:S(2)}) collective-permute-start(f32[256,2,128]{2,0,1:T(8,128)S(1)} %fusion.45), channel_id=1, source_target_pairs={{0,8},{8,16},{16,24},{24,32},{32,40},{40,48},{48,56},{56,64},{64,7... | collective-permute-start | bytes 786440 | tf_op jit(solution)/shard_map/while/body/eval_jaxpr/ppermute | solution.py:12
  87.5 5.3 %collective-permute-done.2 = f32[256,2]{0,1:T(2,128)S(1)} collective-permute-done((f32[256,2]{0,1:T(2,128)S(1)}, f32[256,2]{0,1:T(2,128)S(1)}, u32[]{:S(2)}, u32[]{:S(2)}) %collective-permute-start.2) | collective-permute-done | bytes 2080 | tf_op jit(solution)/shard_map/while/body/eval_jaxpr/ppermute | solution.py:12
  99.9 3.5 fusion.45
  103.4 4.0 collective-permute-start.1
  107.5 5.0 %collective-permute-done.2 = f32[256,2]{0,1:T(2,128)S(1)} collective-permute-done((f32[256,2]{0,1:T(2,128)S(1)}, f32[256,2]{0,1:T(2,128)S(1)}, u32[]{:S(2)}, u32[]{:S(2)}) %collective-permute-start.2) | collective-permute-done | bytes 2080 | tf_op jit(solution)/shard_map/while/body/eval_jaxpr/ppermute | solution.py:12
  119.6 3.5 fusion.45
  123.1 3.7 collective-permute-start.1
  126.9 4.6 %collective-permute-done.2 = f32[256,2]{0,1:T(2,128)S(1)} collective-permute-done((f32[256,2]{0,1:T(2,128)S(1)}, f32[256,2]{0,1:T(2,128)S(1)}, u32[]{:S(2)}, u32[]{:S(2)}) %collective-permute-start.2) | collective-permute-done | bytes 2080 | tf_op jit(solution)/shard_map/while/body/eval_jaxpr/ppermute | solution.py:12
  138.6 3.5 fusion.45
  142.1 4.1 %collective-permute-start.1 = (f32[256,2,128]{2,0,1:T(8,128)S(1)}, f32[256,2,128]{2,0,1:T(8,128)S(1)}, u32[]{:S(2)}, u32[]{:S(2)}) collective-permute-start(f32[256,2,128]{2,0,1:T(8,128)S(1)} %fusion.45), channel_id=1, source_target_pairs={{0,8},{8,16},{16,24},{24,32},{32,40},{40,48},{48,56},{56,64},{64,7... | collective-permute-start | bytes 786440 | tf_op jit(solution)/shard_map/while/body/eval_jaxpr/ppermute | solution.py:12
  146.4 4.7 %collective-permute-done.2 = f32[256,2]{0,1:T(2,128)S(1)} collective-permute-done((f32[256,2]{0,1:T(2,128)S(1)}, f32[256,2]{0,1:T(2,128)S(1)}, u32[]{:S(2)}, u32[]{:S(2)}) %collective-permute-start.2) | collective-permute-done | bytes 2080 | tf_op jit(solution)/shard_map/while/body/eval_jaxpr/ppermute | solution.py:12
  161.6 4.0 collective-permute-start.1
  165.8 5.9 %collective-permute-done.2 = f32[256,2]{0,1:T(2,128)S(1)} collective-permute-done((f32[256,2]{0,1:T(2,128)S(1)}, f32[256,2]{0,1:T(2,128)S(1)}, u32[]{:S(2)}, u32[]{:S(2)}) %collective-permute-start.2) | collective-permute-done | bytes 2080 | tf_op jit(solution)/shard_map/while/body/eval_jaxpr/ppermute | solution.py:12
  185.2 7.1 %collective-permute-done.2 = f32[256,2]{0,1:T(2,128)S(1)} collective-permute-done((f32[256,2]{0,1:T(2,128)S(1)}, f32[256,2]{0,1:T(2,128)S(1)}, u32[]{:S(2)}, u32[]{:S(2)}) %collective-permute-start.2) | collective-permute-done | bytes 2080 | tf_op jit(solution)/shard_map/while/body/eval_jaxpr/ppermute | solution.py:12
  204.6 8.3 %collective-permute-done.2 = f32[256,2]{0,1:T(2,128)S(1)} collective-permute-done((f32[256,2]{0,1:T(2,128)S(1)}, f32[256,2]{0,1:T(2,128)S(1)}, u32[]{:S(2)}, u32[]{:S(2)}) %collective-permute-start.2) | collective-permute-done | bytes 2080 | tf_op jit(solution)/shard_map/while/body/eval_jaxpr/ppermute | solution.py:12
  224.1 9.5 %collective-permute-done.2 = f32[256,2]{0,1:T(2,128)S(1)} collective-permute-done((f32[256,2]{0,1:T(2,128)S(1)}, f32[256,2]{0,1:T(2,128)S(1)}, u32[]{:S(2)}, u32[]{:S(2)}) %collective-permute-start.2) | collective-permute-done | bytes 2080 | tf_op jit(solution)/shard_map/while/body/eval_jaxpr/ppermute | solution.py:12
  244.4 9.8 %collective-permute-done.2 = f32[256,2]{0,1:T(2,128)S(1)} collective-permute-done((f32[256,2]{0,1:T(2,128)S(1)}, f32[256,2]{0,1:T(2,128)S(1)}, u32[]{:S(2)}, u32[]{:S(2)}) %collective-permute-start.2) | collective-permute-done | bytes 2080 | tf_op jit(solution)/shard_map/while/body/eval_jaxpr/ppermute | solution.py:12
  265.0 9.8 %collective-permute-done.2 = f32[256,2]{0,1:T(2,128)S(1)} collective-permute-done((f32[256,2]{0,1:T(2,128)S(1)}, f32[256,2]{0,1:T(2,128)S(1)}, u32[]{:S(2)}, u32[]{:S(2)}) %collective-permute-start.2) | collective-permute-done | bytes 2080 | tf_op jit(solution)/shard_map/while/body/eval_jaxpr/ppermute | solution.py:12
  285.7 9.8 %collective-permute-done.2 = f32[256,2]{0,1:T(2,128)S(1)} collective-permute-done((f32[256,2]{0,1:T(2,128)S(1)}, f32[256,2]{0,1:T(2,128)S(1)}, u32[]{:S(2)}, u32[]{:S(2)}) %collective-permute-start.2) | collective-permute-done | bytes 2080 | tf_op jit(solution)/shard_map/while/body/eval_jaxpr/ppermute | solution.py:12
  306.3 9.8 %collective-permute-done.2 = f32[256,2]{0,1:T(2,128)S(1)} collective-permute-done((f32[256,2]{0,1:T(2,128)S(1)}, f32[256,2]{0,1:T(2,128)S(1)}, u32[]{:S(2)}, u32[]{:S(2)}) %collective-permute-start.2) | collective-permute-done | bytes 2080 | tf_op jit(solution)/shard_map/while/body/eval_jaxpr/ppermute | solution.py:12
  326.9 9.8 %collective-permute-done.2 = f32[256,2]{0,1:T(2,128)S(1)} collective-permute-done((f32[256,2]{0,1:T(2,128)S(1)}, f32[256,2]{0,1:T(2,128)S(1)}, u32[]{:S(2)}, u32[]{:S(2)}) %collective-permute-start.2) | collective-permute-done | bytes 2080 | tf_op jit(solution)/shard_map/while/body/eval_jaxpr/ppermute | solution.py:12
  337.5 50.7 %all-gather.2.cloned.1.call-done = bf16[256,2048]{0,1:T(8,128)(2,1)} async-done(((bf16[256,256]{0,1:T(8,128)(2,1)}), bf16[256,2048]{0,1:T(8,128)(2,1)}) %all-gather.2.cloned.1.call-update) | async-done | bytes 1048592 | tf_op jit(solution)/shard_map/all_gather | solution.py:85
  388.3 7.0 %convolution_convert_fusion = bf16[256,2048]{1,0:T(8,128)(2,1)} fusion(bf16[256,2048]{0,1:T(8,128)(2,1)} %all-gather.2.cloned.1.call-done, bf16[2048,2048]{1,0:T(8,128)(2,1)} %param.11), kind=kOutput, calls=%fused_computation.31 | convolution fusion | flops 2148007936 | bytes 10485760 | tf_op jit(solution)/shard_map/dot_general | solution.py:84
  (273 shorter events, 163.1 us)
Async XLA Ops:
  6.5 381.7 %all-gather.2.cloned.1.call-start = ((), (), s32[]{:S(2)}) async-start(), calls=%async_computation | async-start | bytes 1179648 | tf_op jit(solution)/shard_map/all_gather | solution.py:85
  20.0 10.1 %collective-permute-start.1 = (f32[256,2,128]{2,0,1:T(8,128)S(1)}, f32[256,2,128]{2,0,1:T(8,128)S(1)}, u32[]{:S(2)}, u32[]{:S(2)}) collective-permute-start(f32[256,2,128]{2,0,1:T(8,128)S(1)} %fusion.45), channel_id=1, source_target_pairs={{0,8},{8,16},{16,24},{24,32},{32,40},{40,48},{48,56},{56,64},{64,7... | collective-permute-start | bytes 786440 | tf_op jit(solution)/shard_map/while/body/eval_jaxpr/ppermute | solution.py:12
  21.7 8.5 %collective-permute-start = (bf16[256,256]{1,0:T(8,128)(2,1)S(1)}, bf16[256,256]{1,0:T(8,128)(2,1)S(1)}, u32[]{:S(2)}, u32[]{:S(2)}) collective-permute-start(bf16[256,256]{1,0:T(8,128)(2,1)S(1)} %copy.26), channel_id=1, source_target_pairs={{0,8},{8,16},{16,24},{24,32},{32,40},{40,48},{48,56},{56,64},{64,7... | collective-permute-start | bytes 393224 | tf_op jit(solution)/shard_map/while/body/eval_jaxpr/ppermute | solution.py:12
  40.7 10.7 %collective-permute-start.1 = (f32[256,2,128]{2,0,1:T(8,128)S(1)}, f32[256,2,128]{2,0,1:T(8,128)S(1)}, u32[]{:S(2)}, u32[]{:S(2)}) collective-permute-start(f32[256,2,128]{2,0,1:T(8,128)S(1)} %fusion.45), channel_id=1, source_target_pairs={{0,8},{8,16},{16,24},{24,32},{32,40},{40,48},{48,56},{56,64},{64,7... | collective-permute-start | bytes 786440 | tf_op jit(solution)/shard_map/while/body/eval_jaxpr/ppermute | solution.py:12
  62.0 10.4 %collective-permute-start.1 = (f32[256,2,128]{2,0,1:T(8,128)S(1)}, f32[256,2,128]{2,0,1:T(8,128)S(1)}, u32[]{:S(2)}, u32[]{:S(2)}) collective-permute-start(f32[256,2,128]{2,0,1:T(8,128)S(1)} %fusion.45), channel_id=1, source_target_pairs={{0,8},{8,16},{16,24},{24,32},{32,40},{40,48},{48,56},{56,64},{64,7... | collective-permute-start | bytes 786440 | tf_op jit(solution)/shard_map/while/body/eval_jaxpr/ppermute | solution.py:12
  82.9 9.9 %collective-permute-start.1 = (f32[256,2,128]{2,0,1:T(8,128)S(1)}, f32[256,2,128]{2,0,1:T(8,128)S(1)}, u32[]{:S(2)}, u32[]{:S(2)}) collective-permute-start(f32[256,2,128]{2,0,1:T(8,128)S(1)} %fusion.45), channel_id=1, source_target_pairs={{0,8},{8,16},{16,24},{24,32},{32,40},{40,48},{48,56},{56,64},{64,7... | collective-permute-start | bytes 786440 | tf_op jit(solution)/shard_map/while/body/eval_jaxpr/ppermute | solution.py:12
  103.4 9.1 %collective-permute-start.1 = (f32[256,2,128]{2,0,1:T(8,128)S(1)}, f32[256,2,128]{2,0,1:T(8,128)S(1)}, u32[]{:S(2)}, u32[]{:S(2)}) collective-permute-start(f32[256,2,128]{2,0,1:T(8,128)S(1)} %fusion.45), channel_id=1, source_target_pairs={{0,8},{8,16},{16,24},{24,32},{32,40},{40,48},{48,56},{56,64},{64,7... | collective-permute-start | bytes 786440 | tf_op jit(solution)/shard_map/while/body/eval_jaxpr/ppermute | solution.py:12
  123.1 8.4 %collective-permute-start.1 = (f32[256,2,128]{2,0,1:T(8,128)S(1)}, f32[256,2,128]{2,0,1:T(8,128)S(1)}, u32[]{:S(2)}, u32[]{:S(2)}) collective-permute-start(f32[256,2,128]{2,0,1:T(8,128)S(1)} %fusion.45), channel_id=1, source_target_pairs={{0,8},{8,16},{16,24},{24,32},{32,40},{40,48},{48,56},{56,64},{64,7... | collective-permute-start | bytes 786440 | tf_op jit(solution)/shard_map/while/body/eval_jaxpr/ppermute | solution.py:12
  142.1 8.9 %collective-permute-start.1 = (f32[256,2,128]{2,0,1:T(8,128)S(1)}, f32[256,2,128]{2,0,1:T(8,128)S(1)}, u32[]{:S(2)}, u32[]{:S(2)}) collective-permute-start(f32[256,2,128]{2,0,1:T(8,128)S(1)} %fusion.45), channel_id=1, source_target_pairs={{0,8},{8,16},{16,24},{24,32},{32,40},{40,48},{48,56},{56,64},{64,7... | collective-permute-start | bytes 786440 | tf_op jit(solution)/shard_map/while/body/eval_jaxpr/ppermute | solution.py:12
  161.6 10.0 %collective-permute-start.1 = (f32[256,2,128]{2,0,1:T(8,128)S(1)}, f32[256,2,128]{2,0,1:T(8,128)S(1)}, u32[]{:S(2)}, u32[]{:S(2)}) collective-permute-start(f32[256,2,128]{2,0,1:T(8,128)S(1)} %fusion.45), channel_id=1, source_target_pairs={{0,8},{8,16},{16,24},{24,32},{32,40},{40,48},{48,56},{56,64},{64,7... | collective-permute-start | bytes 786440 | tf_op jit(solution)/shard_map/while/body/eval_jaxpr/ppermute | solution.py:12
  182.3 10.0 %collective-permute-start.1 = (f32[256,2,128]{2,0,1:T(8,128)S(1)}, f32[256,2,128]{2,0,1:T(8,128)S(1)}, u32[]{:S(2)}, u32[]{:S(2)}) collective-permute-start(f32[256,2,128]{2,0,1:T(8,128)S(1)} %fusion.45), channel_id=1, source_target_pairs={{0,8},{8,16},{16,24},{24,32},{32,40},{40,48},{48,56},{56,64},{64,7... | collective-permute-start | bytes 786440 | tf_op jit(solution)/shard_map/while/body/eval_jaxpr/ppermute | solution.py:12
  202.9 10.1 %collective-permute-start.1 = (f32[256,2,128]{2,0,1:T(8,128)S(1)}, f32[256,2,128]{2,0,1:T(8,128)S(1)}, u32[]{:S(2)}, u32[]{:S(2)}) collective-permute-start(f32[256,2,128]{2,0,1:T(8,128)S(1)} %fusion.45), channel_id=1, source_target_pairs={{0,8},{8,16},{16,24},{24,32},{32,40},{40,48},{48,56},{56,64},{64,7... | collective-permute-start | bytes 786440 | tf_op jit(solution)/shard_map/while/body/eval_jaxpr/ppermute | solution.py:12
  204.5 8.5 %collective-permute-start = (bf16[256,256]{1,0:T(8,128)(2,1)S(1)}, bf16[256,256]{1,0:T(8,128)(2,1)S(1)}, u32[]{:S(2)}, u32[]{:S(2)}) collective-permute-start(bf16[256,256]{1,0:T(8,128)(2,1)S(1)} %copy.26), channel_id=1, source_target_pairs={{0,8},{8,16},{16,24},{24,32},{32,40},{40,48},{48,56},{56,64},{64,7... | collective-permute-start | bytes 393224 | tf_op jit(solution)/shard_map/while/body/eval_jaxpr/ppermute | solution.py:12
  204.5 8.4 %collective-permute-start.2 = (f32[256,2]{0,1:T(2,128)S(1)}, f32[256,2]{0,1:T(2,128)S(1)}, u32[]{:S(2)}, u32[]{:S(2)}) collective-permute-start(f32[256,2]{0,1:T(2,128)S(1)} %get-tuple-element.382), channel_id=1, source_target_pairs={{0,8},{8,16},{16,24},{24,32},{32,40},{40,48},{48,56},{56,64},{64,7... | collective-permute-start | bytes 6152 | tf_op jit(solution)/shard_map/while/body/eval_jaxpr/ppermute | solution.py:12
  223.5 10.0 %collective-permute-start.1 = (f32[256,2,128]{2,0,1:T(8,128)S(1)}, f32[256,2,128]{2,0,1:T(8,128)S(1)}, u32[]{:S(2)}, u32[]{:S(2)}) collective-permute-start(f32[256,2,128]{2,0,1:T(8,128)S(1)} %fusion.45), channel_id=1, source_target_pairs={{0,8},{8,16},{16,24},{24,32},{32,40},{40,48},{48,56},{56,64},{64,7... | collective-permute-start | bytes 786440 | tf_op jit(solution)/shard_map/while/body/eval_jaxpr/ppermute | solution.py:12
  223.9 9.7 %collective-permute-start = (bf16[256,256]{1,0:T(8,128)(2,1)S(1)}, bf16[256,256]{1,0:T(8,128)(2,1)S(1)}, u32[]{:S(2)}, u32[]{:S(2)}) collective-permute-start(bf16[256,256]{1,0:T(8,128)(2,1)S(1)} %copy.26), channel_id=1, source_target_pairs={{0,8},{8,16},{16,24},{24,32},{32,40},{40,48},{48,56},{56,64},{64,7... | collective-permute-start | bytes 393224 | tf_op jit(solution)/shard_map/while/body/eval_jaxpr/ppermute | solution.py:12
  224.0 9.6 %collective-permute-start.2 = (f32[256,2]{0,1:T(2,128)S(1)}, f32[256,2]{0,1:T(2,128)S(1)}, u32[]{:S(2)}, u32[]{:S(2)}) collective-permute-start(f32[256,2]{0,1:T(2,128)S(1)} %get-tuple-element.382), channel_id=1, source_target_pairs={{0,8},{8,16},{16,24},{24,32},{32,40},{40,48},{48,56},{56,64},{64,7... | collective-permute-start | bytes 6152 | tf_op jit(solution)/shard_map/while/body/eval_jaxpr/ppermute | solution.py:12
  244.2 10.0 %collective-permute-start.1 = (f32[256,2,128]{2,0,1:T(8,128)S(1)}, f32[256,2,128]{2,0,1:T(8,128)S(1)}, u32[]{:S(2)}, u32[]{:S(2)}) collective-permute-start(f32[256,2,128]{2,0,1:T(8,128)S(1)} %fusion.45), channel_id=1, source_target_pairs={{0,8},{8,16},{16,24},{24,32},{32,40},{40,48},{48,56},{56,64},{64,7... | collective-permute-start | bytes 786440 | tf_op jit(solution)/shard_map/while/body/eval_jaxpr/ppermute | solution.py:12
  244.2 10.0 %collective-permute-start = (bf16[256,256]{1,0:T(8,128)(2,1)S(1)}, bf16[256,256]{1,0:T(8,128)(2,1)S(1)}, u32[]{:S(2)}, u32[]{:S(2)}) collective-permute-start(bf16[256,256]{1,0:T(8,128)(2,1)S(1)} %copy.26), channel_id=1, source_target_pairs={{0,8},{8,16},{16,24},{24,32},{32,40},{40,48},{48,56},{56,64},{64,7... | collective-permute-start | bytes 393224 | tf_op jit(solution)/shard_map/while/body/eval_jaxpr/ppermute | solution.py:12
  244.3 9.9 %collective-permute-start.2 = (f32[256,2]{0,1:T(2,128)S(1)}, f32[256,2]{0,1:T(2,128)S(1)}, u32[]{:S(2)}, u32[]{:S(2)}) collective-permute-start(f32[256,2]{0,1:T(2,128)S(1)} %get-tuple-element.382), channel_id=1, source_target_pairs={{0,8},{8,16},{16,24},{24,32},{32,40},{40,48},{48,56},{56,64},{64,7... | collective-permute-start | bytes 6152 | tf_op jit(solution)/shard_map/while/body/eval_jaxpr/ppermute | solution.py:12
  264.8 10.1 %collective-permute-start.1 = (f32[256,2,128]{2,0,1:T(8,128)S(1)}, f32[256,2,128]{2,0,1:T(8,128)S(1)}, u32[]{:S(2)}, u32[]{:S(2)}) collective-permute-start(f32[256,2,128]{2,0,1:T(8,128)S(1)} %fusion.45), channel_id=1, source_target_pairs={{0,8},{8,16},{16,24},{24,32},{32,40},{40,48},{48,56},{56,64},{64,7... | collective-permute-start | bytes 786440 | tf_op jit(solution)/shard_map/while/body/eval_jaxpr/ppermute | solution.py:12
  264.9 10.0 %collective-permute-start = (bf16[256,256]{1,0:T(8,128)(2,1)S(1)}, bf16[256,256]{1,0:T(8,128)(2,1)S(1)}, u32[]{:S(2)}, u32[]{:S(2)}) collective-permute-start(bf16[256,256]{1,0:T(8,128)(2,1)S(1)} %copy.26), channel_id=1, source_target_pairs={{0,8},{8,16},{16,24},{24,32},{32,40},{40,48},{48,56},{56,64},{64,7... | collective-permute-start | bytes 393224 | tf_op jit(solution)/shard_map/while/body/eval_jaxpr/ppermute | solution.py:12
  265.0 9.9 %collective-permute-start.2 = (f32[256,2]{0,1:T(2,128)S(1)}, f32[256,2]{0,1:T(2,128)S(1)}, u32[]{:S(2)}, u32[]{:S(2)}) collective-permute-start(f32[256,2]{0,1:T(2,128)S(1)} %get-tuple-element.382), channel_id=1, source_target_pairs={{0,8},{8,16},{16,24},{24,32},{32,40},{40,48},{48,56},{56,64},{64,7... | collective-permute-start | bytes 6152 | tf_op jit(solution)/shard_map/while/body/eval_jaxpr/ppermute | solution.py:12
  285.4 10.0 %collective-permute-start.1 = (f32[256,2,128]{2,0,1:T(8,128)S(1)}, f32[256,2,128]{2,0,1:T(8,128)S(1)}, u32[]{:S(2)}, u32[]{:S(2)}) collective-permute-start(f32[256,2,128]{2,0,1:T(8,128)S(1)} %fusion.45), channel_id=1, source_target_pairs={{0,8},{8,16},{16,24},{24,32},{32,40},{40,48},{48,56},{56,64},{64,7... | collective-permute-start | bytes 786440 | tf_op jit(solution)/shard_map/while/body/eval_jaxpr/ppermute | solution.py:12
  285.5 10.0 %collective-permute-start = (bf16[256,256]{1,0:T(8,128)(2,1)S(1)}, bf16[256,256]{1,0:T(8,128)(2,1)S(1)}, u32[]{:S(2)}, u32[]{:S(2)}) collective-permute-start(bf16[256,256]{1,0:T(8,128)(2,1)S(1)} %copy.26), channel_id=1, source_target_pairs={{0,8},{8,16},{16,24},{24,32},{32,40},{40,48},{48,56},{56,64},{64,7... | collective-permute-start | bytes 393224 | tf_op jit(solution)/shard_map/while/body/eval_jaxpr/ppermute | solution.py:12
  285.6 9.9 %collective-permute-start.2 = (f32[256,2]{0,1:T(2,128)S(1)}, f32[256,2]{0,1:T(2,128)S(1)}, u32[]{:S(2)}, u32[]{:S(2)}) collective-permute-start(f32[256,2]{0,1:T(2,128)S(1)} %get-tuple-element.382), channel_id=1, source_target_pairs={{0,8},{8,16},{16,24},{24,32},{32,40},{40,48},{48,56},{56,64},{64,7... | collective-permute-start | bytes 6152 | tf_op jit(solution)/shard_map/while/body/eval_jaxpr/ppermute | solution.py:12
  306.1 10.0 %collective-permute-start.1 = (f32[256,2,128]{2,0,1:T(8,128)S(1)}, f32[256,2,128]{2,0,1:T(8,128)S(1)}, u32[]{:S(2)}, u32[]{:S(2)}) collective-permute-start(f32[256,2,128]{2,0,1:T(8,128)S(1)} %fusion.45), channel_id=1, source_target_pairs={{0,8},{8,16},{16,24},{24,32},{32,40},{40,48},{48,56},{56,64},{64,7... | collective-permute-start | bytes 786440 | tf_op jit(solution)/shard_map/while/body/eval_jaxpr/ppermute | solution.py:12
  306.1 10.0 %collective-permute-start = (bf16[256,256]{1,0:T(8,128)(2,1)S(1)}, bf16[256,256]{1,0:T(8,128)(2,1)S(1)}, u32[]{:S(2)}, u32[]{:S(2)}) collective-permute-start(bf16[256,256]{1,0:T(8,128)(2,1)S(1)} %copy.26), channel_id=1, source_target_pairs={{0,8},{8,16},{16,24},{24,32},{32,40},{40,48},{48,56},{56,64},{64,7... | collective-permute-start | bytes 393224 | tf_op jit(solution)/shard_map/while/body/eval_jaxpr/ppermute | solution.py:12
  306.2 9.9 %collective-permute-start.2 = (f32[256,2]{0,1:T(2,128)S(1)}, f32[256,2]{0,1:T(2,128)S(1)}, u32[]{:S(2)}, u32[]{:S(2)}) collective-permute-start(f32[256,2]{0,1:T(2,128)S(1)} %get-tuple-element.382), channel_id=1, source_target_pairs={{0,8},{8,16},{16,24},{24,32},{32,40},{40,48},{48,56},{56,64},{64,7... | collective-permute-start | bytes 6152 | tf_op jit(solution)/shard_map/while/body/eval_jaxpr/ppermute | solution.py:12
  326.7 10.1 %collective-permute-start.1 = (f32[256,2,128]{2,0,1:T(8,128)S(1)}, f32[256,2,128]{2,0,1:T(8,128)S(1)}, u32[]{:S(2)}, u32[]{:S(2)}) collective-permute-start(f32[256,2,128]{2,0,1:T(8,128)S(1)} %fusion.45), channel_id=1, source_target_pairs={{0,8},{8,16},{16,24},{24,32},{32,40},{40,48},{48,56},{56,64},{64,7... | collective-permute-start | bytes 786440 | tf_op jit(solution)/shard_map/while/body/eval_jaxpr/ppermute | solution.py:12
  326.8 10.0 %collective-permute-start = (bf16[256,256]{1,0:T(8,128)(2,1)S(1)}, bf16[256,256]{1,0:T(8,128)(2,1)S(1)}, u32[]{:S(2)}, u32[]{:S(2)}) collective-permute-start(bf16[256,256]{1,0:T(8,128)(2,1)S(1)} %copy.26), channel_id=1, source_target_pairs={{0,8},{8,16},{16,24},{24,32},{32,40},{40,48},{48,56},{56,64},{64,7... | collective-permute-start | bytes 393224 | tf_op jit(solution)/shard_map/while/body/eval_jaxpr/ppermute | solution.py:12
  326.9 9.9 %collective-permute-start.2 = (f32[256,2]{0,1:T(2,128)S(1)}, f32[256,2]{0,1:T(2,128)S(1)}, u32[]{:S(2)}, u32[]{:S(2)}) collective-permute-start(f32[256,2]{0,1:T(2,128)S(1)} %get-tuple-element.382), channel_id=1, source_target_pairs={{0,8},{8,16},{16,24},{24,32},{32,40},{40,48},{48,56},{56,64},{64,7... | collective-permute-start | bytes 6152 | tf_op jit(solution)/shard_map/while/body/eval_jaxpr/ppermute | solution.py:12
  (33 other events, 194.8 us)
Sparse Core Ops, SparseCore 0:
  337.7 50.5 all-gather.1
where the time goes:
time: 404 us; the launch traced here: 402 us
  waiting for transfers between devices  169 us (42%)
  matrix products  115 us (28%)
  other arithmetic  62.4 us (15%)
  starting transfers between devices  39.8 us (10%)
  between operations  13.4 us (3%)
    ppermute x48, waiting for transfers between devices, from_behind(): return lax.ppermute(value, axis, pairs)  118 us
    dot_general x16, matrix products, partial_block(): jnp.einsum('nhk,kd->nhd', weights.astype(jnp.bfloat16), value_rows, prefe...  55.8 us
    dot_general x16, matrix products, partial_block(): jnp.einsum('nhd,kd->nhk', q_three, key_rows, preferred_element_type=jnp.f...  52.1 us
    all_gather x1, waiting for transfers between devices, body(): lax.all_gather(attended, 'head', axis=1, tiled=True)  50.7 us
    reduce_sum x16, other arithmetic, partial_block(): total = jnp.sum(weights, axis=2)  42.5 us
    ppermute x48, starting transfers between devices, from_behind(): return lax.ppermute(value, axis, pairs)  39.8 us
    and x16, other arithmetic, partial_block(): (q_req[:, None] == k_req[None, :]) & (k_pos[None, :] <= q_pos[:, None])  14.7 us
  transfers between devices with their start and end apart: 49, of which 17 were waited for; matrix products, arithmetic and copies ran while one was open for 0% of the time, Pallas kernels for 0%

commit v1 on v0

v1 whole, which is shorter than its diff:
```python
import functools
import math

import jax
import jax.numpy as jnp
from jax import lax
from jax.experimental import pallas as pl
from jax.experimental.pallas import tpu as pltpu
from jax.sharding import PartitionSpec as P

MESH = pl.DeviceIdType.MESH
CTX = 16
HEAD = 8
SIDE = 4
REQS = 8
HALF = 128
WIDTH = 128
HEADS = 2
LANES = HALF * HEADS
KEYS = 4096
PIECE = KEYS // HEAD
TILE = 512
SUB = 256
SUMS = 16
LOW = -1e9
NEG = -1e30
LARGE = 2.0**100
SCALE = math.log2(math.e) / math.sqrt(WIDTH)
VMEM = 56 * 1024 * 1024


def remote(src, dst, send, recv, ctx, head):
    return pltpu.make_async_remote_copy(
        src_ref=src, dst_ref=dst, send_sem=send, recv_sem=recv, device_id=(ctx, head), device_id_type=MESH
    )


def greet(peers):
    barrier = pltpu.get_barrier_semaphore()
    for ctx, head in peers:
        pl.semaphore_signal(barrier, inc=1, device_id=(ctx, head), device_id_type=MESH)
    pl.semaphore_wait(barrier, len(peers))


def dispatch_kernel(
    q_ref, k_ref, v_ref, qg_ref, ko_ref, vo_ref, own_sem, qz_send, qx_send, q_recv, kz_send, ky_send, kc_send, k_recv
):
    ctx, head = lax.axis_index("ctx"), lax.axis_index("head")
    z, x = ctx // SIDE, ctx % SIDE
    y, core = head // 2, head % 2
    far = lax.rem(ctx + CTX // 2, CTX)
    twin = y * 2 + (1 - core)

    def zed(d):
        return lax.rem(z + d, SIDE)

    def on_x(d):
        return z * SIDE + lax.rem(x + d, SIDE)

    def on_y(d):
        return lax.rem(y + d, SIDE) * 2 + core

    greet(
        [(zed(d) * SIDE + x, head) for d in (1, 2, 3)]
        + [(on_x(d), head) for d in (1, 2, 3)]
        + [(ctx, on_y(d)) for d in (1, 2, 3)]
        + [(ctx, twin)]
    )
    cache = (k_ref, v_ref)
    far_cache = (ko_ref, vo_ref)
    pending = []

    def start(copy):
        copy.start()
        pending.append(copy)
        return copy

    def piece(ref, p):
        return ref.at[pl.ds(p * PIECE, PIECE), :]

    def rows(zt):
        return q_ref.at[pl.ds((zt // 2) * HALF, HALF), :]

    def share_q(slot, src, turn):
        for d in (1, 3, 2):
            start(remote(src, qg_ref.at[slot], qx_send.at[turn, d - 1], q_recv.at[slot], on_x(d), head))

    for i in range(2):
        start(remote(piece(cache[i], head), piece(far_cache[i], head), kz_send.at[i], k_recv.at[i, head], far, head))
    for d in (1, 3, 2):
        zt = zed(d)
        start(remote(rows(zt), qg_ref.at[ctx], qz_send.at[d - 1], q_recv.at[ctx], zt * SIDE + x, head))
    own = pltpu.make_async_copy(rows(z), qg_ref.at[ctx], own_sem)
    own.start()
    share_q(ctx, rows(z), 0)

    def arrived_q(slot):
        remote(qg_ref.at[slot], qg_ref.at[slot], qz_send.at[0], q_recv.at[slot], ctx, head).wait_recv()

    def arrived_kv(i, p):
        ref = piece(far_cache[i], p)
        remote(ref, ref, kz_send.at[0], k_recv.at[i, p], ctx, head).wait_recv()

    def pass_q(d):
        slot = zed(d) * SIDE + x
        arrived_q(slot)
        share_q(slot, qg_ref.at[slot], d)

    def pass_kv(i):
        arrived_kv(i, head)
        ref = piece(far_cache[i], head)
        for d in (1, 3, 2):
            start(remote(ref, ref, ky_send.at[i, d - 1], k_recv.at[i, head], ctx, on_y(d)))
        start(remote(ref, ref, kc_send.at[i, 0], k_recv.at[i, head], ctx, twin))

    pass_q(1)
    pass_q(3)
    pass_kv(0)
    pass_q(2)
    pass_kv(1)
    for i in range(2):
        for d in (1, 3, 2):
            p = on_y(d)
            arrived_kv(i, p)
            ref = piece(far_cache[i], p)
            start(remote(ref, ref, kc_send.at[i, d], k_recv.at[i, p], ctx, twin))
    for dx in (1, 2, 3):
        for dz in range(SIDE):
            arrived_q(zed(dz) * SIDE + lax.rem(x + dx, SIDE))
    for i in range(2):
        for d in range(SIDE):
            arrived_kv(i, lax.rem(y + d, SIDE) * 2 + (1 - core))
    own.wait()
    for copy in pending:
        copy.wait_send()


def dispatch(queries, keys, values):
    anywhere = pl.BlockSpec(memory_space=pl.ANY)
    dma = pltpu.SemaphoreType.DMA
    return pl.pallas_call(
        dispatch_kernel,
        out_shape=(
            jax.ShapeDtypeStruct((CTX, HALF, LANES), queries.dtype),
            jax.ShapeDtypeStruct(keys.shape, keys.dtype),
            jax.ShapeDtypeStruct(values.shape, values.dtype),
        ),
        in_specs=[anywhere] * 3,
        out_specs=(anywhere,) * 3,
        scratch_shapes=[
            dma,
            dma((3,)),
            dma((SIDE, 3)),
            dma((CTX,)),
            dma((2,)),
            dma((2, 3)),
            dma((2, SIDE)),
            dma((2, HEAD)),
        ],
        compiler_params=pltpu.CompilerParams(collective_id=0, has_side_effects=True),
        name="dispatch",
    )(queries, keys, values)


def attend_kernel(new_ref, prior_ref, qg_ref, k_ref, v_ref, ko_ref, vo_ref, ot_ref, st_ref, vt_ref, qt_ref, m_ref, acc_ref, bad_ref):
    ctx = lax.axis_index("ctx")
    half = ctx // (CTX // 2)
    far = lax.rem(ctx + CTX // 2, CTX)
    vt_ref[WIDTH:, :] = jnp.ones((SUMS, 2 * KEYS), jnp.bfloat16)
    for part, ref in enumerate((v_ref, vo_ref)):

        @pl.loop(0, KEYS // TILE)
        def _(t):
            at = pl.multiple_of(t * TILE, TILE)
            to = pl.multiple_of(part * KEYS + t * TILE, TILE)
            vt_ref[:WIDTH, pl.ds(to, TILE)] = ref[pl.ds(at, TILE), :].T

    q_start, k_start = [jnp.int32(0)], [jnp.int32(0)]
    for r in range(REQS - 1):
        q_start.append(q_start[-1] + new_ref[r])
        k_start.append(k_start[-1] + new_ref[r] + prior_ref[r])

    def bounds(row):
        lo = jnp.zeros_like(row)
        hi = row + prior_ref[0]
        for r in range(1, REQS):
            here = row >= q_start[r]
            lo = jnp.where(here, k_start[r], lo)
            hi = jnp.where(here, row - q_start[r] + prior_ref[r] + k_start[r], hi)
        return lo, hi

    lane = lax.broadcasted_iota(jnp.int32, (1, LANES), 1) % HALF
    bases = (ctx * KEYS, far * KEYS)

    @pl.loop(0, CTX)
    def _(b):
        first = b * (2 * HALF) + half * HALF
        last = first + HALF - 1
        lo_all, full_hi = bounds(first)
        full_lo, hi_all = bounds(last)
        spans = []
        for base in bases:
            begin = jnp.clip(lo_all - base, 0, KEYS)
            end = jnp.clip(hi_all + 1 - base, 0, KEYS)
            spans.append((begin // TILE, jnp.where(end > begin, (end + TILE - 1) // TILE, begin // TILE)))
        some = (spans[0][1] > spans[0][0]) | (spans[1][1] > spans[1][0])

        @pl.when(jnp.logical_not(some))
        def _():
            ot_ref[b] = jnp.zeros((WIDTH, LANES), ot_ref.dtype)
            st_ref[b] = jnp.full((8, LANES), NEG, jnp.float32)

        @pl.when(some)
        def _():
            row_lo, row_hi = bounds(first + lane)
            for h in range(HEADS):
                wide = qg_ref[b, :, h * WIDTH : (h + 1) * WIDTH].astype(jnp.float32).T * SCALE
                high = wide.astype(jnp.bfloat16)
                qt_ref[:WIDTH, h * HALF : (h + 1) * HALF] = high
                qt_ref[WIDTH:, h * HALF : (h + 1) * HALF] = (wide - high.astype(jnp.float32)).astype(jnp.bfloat16)
            bad_ref[0] = jnp.int32(1)

            @pl.loop(0, 2)
            def _(attempt):
                @pl.when(bad_ref[0] == 1)
                def _():
                    m_ref[...] = jnp.full((8, LANES), LOW, jnp.float32)
                    acc_ref[...] = jnp.zeros_like(acc_ref)
                    bad_ref[1] = jnp.int32(0)

                    for part, (kr, base) in enumerate(zip((k_ref, ko_ref), bases)):

                        @pl.loop(spans[part][0], spans[part][1])
                        def _(t):
                            at = pl.multiple_of(t * TILE, TILE)
                            to = pl.multiple_of(part * KEYS + t * TILE, TILE)
                            begin = base + at
                            full = (begin >= full_lo) & (begin + TILE - 1 <= full_hi)
                            quick = full & (attempt == 0) & (bad_ref[1] == 1)

                            def scores(j):
                                kk = kr[pl.ds(at + j * SUB, SUB), :]
                                return jnp.dot(
                                    jnp.concatenate([kk, kk], axis=1), qt_ref[...], preferred_element_type=jnp.float32
                                )

                            def weigh(j, p):
                                return jnp.dot(
                                    vt_ref[:, pl.ds(to + j * SUB, SUB)],
                                    p.astype(jnp.bfloat16),
                                    preferred_element_type=jnp.float32,
                                )

                            @pl.when(quick)
                            def _():
                                m = m_ref[0:1, :]
                                total = acc_ref[...]
                                for j in range(TILE // SUB):
                                    total += weigh(j, jnp.exp2(scores(j) - m))
                                acc_ref[...] = total

                            @pl.when(jnp.logical_not(quick))
                            def _():
                                m_old = m_ref[0:1, :]
                                m = m_old
                                held = []
                                for j in range(TILE // SUB):
                                    s = scores(j)
                                    at_key = begin + j * SUB + lax.broadcasted_iota(jnp.int32, (SUB, LANES), 0)
                                    s = jnp.where((at_key >= row_lo) & (at_key <= row_hi), s, NEG)
                                    m = jnp.maximum(m, jnp.max(s, axis=0, keepdims=True))
                                    held.append(s)
                                total = acc_ref[...] * jnp.exp2(m_old - m)
                                for j in range(TILE // SUB):
                                    total += weigh(j, jnp.exp2(held[j] - m))
                                acc_ref[...] = total
                                m_ref[...] = jnp.broadcast_to(m, (8, LANES))
                                bad_ref[1] = jnp.int32(1)

                    fine = jnp.max(jnp.where(acc_ref[WIDTH : WIDTH + 8, :] < LARGE, 0.0, 1.0))
                    bad_ref[0] = jnp.where(fine > 0.0, 1, 0).astype(jnp.int32)

            total = acc_ref[WIDTH : WIDTH + 8, :]
            live = total > 0.0
            safe = jnp.where(live, total, 1.0)
            st_ref[b] = jnp.where(live, m_ref[...] + jnp.log2(safe), NEG)
            ot_ref[b] = (acc_ref[:WIDTH, :] * (1.0 / safe[0:1, :])).astype(ot_ref.dtype)


def attend(new_counts, prior_lengths, gathered, keys, values, far_keys, far_values):
    scalars = pl.BlockSpec(memory_space=pltpu.SMEM)
    vector = pl.BlockSpec(memory_space=pltpu.VMEM)
    return pl.pallas_call(
        attend_kernel,
        out_shape=(
            jax.ShapeDtypeStruct((CTX, WIDTH, LANES), jnp.bfloat16),
            jax.ShapeDtypeStruct((CTX, 8, LANES), jnp.float32),
        ),
        in_specs=[scalars] * 2 + [vector] * 5,
        out_specs=(vector, vector),
        scratch_shapes=[
            pltpu.VMEM((WIDTH + SUMS, 2 * KEYS), jnp.bfloat16),
            pltpu.VMEM((2 * WIDTH, LANES), jnp.bfloat16),
            pltpu.VMEM((8, LANES), jnp.float32),
            pltpu.VMEM((WIDTH + SUMS, LANES), jnp.float32),
            pltpu.SMEM((2,), jnp.int32),
        ],
        compiler_params=pltpu.CompilerParams(vmem_limit_bytes=VMEM),
        name="attend",
    )(new_counts, prior_lengths, gathered, keys, values, far_keys, far_values)


def combine_kernel(
    ot_ref, st_ref, att_ref, og_ref, sg_ref, own_sem, o_send, s_send, o_recv, s_recv, y_send, c_send, a_recv
):
    ctx, head = lax.axis_index("ctx"), lax.axis_index("head")
    y, core = head // 2, head % 2
    twin = y * 2 + (1 - core)

    def on_y(d):
        return lax.rem(y + d, SIDE) * 2 + core

    greet(
        [(lax.rem(ctx + d, CTX), head) for d in range(1, CTX)]
        + [(ctx, on_y(d)) for d in (1, 2, 3)]
        + [(ctx, twin)]
    )
    pending = []

    def start(copy):
        copy.start()
        pending.append(copy)

    for d in range(1, CTX):
        to = lax.rem(ctx + d, CTX)
        start(remote(st_ref.at[to], sg_ref.at[ctx], s_send.at[d], s_recv.at[ctx], to, head))
        start(remote(ot_ref.at[to], og_ref.at[ctx], o_send.at[d], o_recv.at[ctx], to, head))
    own = [
        pltpu.make_async_copy(ot_ref.at[ctx], og_ref.at[ctx], own_sem.at[0]),
        pltpu.make_async_copy(st_ref.at[ctx], sg_ref.at[ctx], own_sem.at[1]),
    ]
    for copy in own:
        copy.start()
    for copy in own:
        copy.wait()
    for d in range(1, CTX):
        of = lax.rem(ctx + d, CTX)
        remote(sg_ref.at[of], sg_ref.at[of], s_send.at[0], s_recv.at[of], ctx, head).wait_recv()
        remote(og_ref.at[of], og_ref.at[of], o_send.at[0], o_recv.at[of], ctx, head).wait_recv()

    def slot(p):
        return att_ref.at[:, pl.ds(pl.multiple_of(p * LANES, LANES), LANES)]

    mine = slot(head)
    for half in range(2):
        members = range(half * CTX // 2, (half + 1) * CTX // 2)
        top = sg_ref[members[0], 0:1, :]
        for i in members[1:]:
            top = jnp.maximum(top, sg_ref[i, 0:1, :])
        shares = [jnp.exp2(sg_ref[i, 0:1, :] - top) for i in members]
        inverse = 1.0 / functools.reduce(jnp.add, shares)
        out = jnp.zeros((WIDTH, LANES), jnp.float32)
        for i, share in zip(members, shares):
            out += og_ref[i].astype(jnp.float32) * (share * inverse)
        for h in range(HEADS):
            mine[half * HALF : (half + 1) * HALF, h * WIDTH : (h + 1) * WIDTH] = (
                out[:, h * HALF : (h + 1) * HALF].T.astype(att_ref.dtype)
            )

    for d in (1, 3, 2):
        start(remote(mine, mine, y_send.at[d - 1], a_recv.at[head], ctx, on_y(d)))
    start(remote(mine, mine, c_send.at[0], a_recv.at[head], ctx, twin))

    def arrived(p):
        remote(slot(p), slot(p), c_send.at[0], a_recv.at[p], ctx, head).wait_recv()

    for d in (1, 3, 2):
        p = on_y(d)
        arrived(p)
        start(remote(slot(p), slot(p), c_send.at[d], a_recv.at[p], ctx, twin))
    for d in range(SIDE):
        arrived(lax.rem(y + d, SIDE) * 2 + (1 - core))
    for copy in pending:
        copy.wait_send()


def combine(outs, logs):
    anywhere = pl.BlockSpec(memory_space=pl.ANY)
    dma = pltpu.SemaphoreType.DMA
    return pl.pallas_call(
        combine_kernel,
        out_shape=jax.ShapeDtypeStruct((2 * HALF, HEAD * LANES), outs.dtype),
        in_specs=[anywhere] * 2,
        out_specs=pl.BlockSpec(memory_space=pltpu.VMEM),
        scratch_shapes=[
            pltpu.VMEM(outs.shape, outs.dtype),
            pltpu.VMEM(logs.shape, logs.dtype),
            dma((2,)),
            dma((CTX,)),
            dma((CTX,)),
            dma((CTX,)),
            dma((CTX,)),
            dma((3,)),
            dma((SIDE,)),
            dma((HEAD,)),
        ],
        compiler_params=pltpu.CompilerParams(collective_id=1, has_side_effects=True, vmem_limit_bytes=VMEM),
        name="combine",
    )(outs, logs)


def body(queries, keys, values, w_out, new_counts, prior_lengths):
    gathered, far_keys, far_values = dispatch(queries, keys, values)
    outs, logs = attend(new_counts, prior_lengths, gathered, keys, values, far_keys, far_values)
    attended = combine(outs, logs)
    return jnp.dot(attended, w_out, preferred_element_type=jnp.float32).astype(jnp.bfloat16)


def solution(mesh):
    return jax.shard_map(
        body,
        mesh=mesh,
        in_specs=(P("ctx", "head"), P("ctx", None), P("ctx", None), P(None, "head"), P(), P()),
        out_specs=P("ctx", "head"),
        check_vma=False,
    )
```

time: 404 us -> 119 us (0.29)
  the two profiles are of different devices: /device:TPU:7 before, /device:TPU:1 now
where the time goes in v1:
time: 119 us
  Pallas kernels  112 us (94%)
  matrix products  7.02 us (6%)
    pallas_call x1, Pallas kernels, attend(): pl.pallas_call(attend_kernel, out_shape=(jax.ShapeDtypeStruct((CTX, WIDTH...  46.7 us
    pallas_call x1, Pallas kernels, dispatch(): pl.pallas_call(dispatch_kernel, out_shape=(jax.ShapeDtypeStruct((CTX, HAL...  34.3 us
    pallas_call x1, Pallas kernels, combine(): pl.pallas_call(combine_kernel, out_shape=jax.ShapeDtypeStruct((2 * HALF,...  30.8 us
    dot_general x1, matrix products, body(): jnp.dot(attended, w_out, preferred_element_type=jnp.float32)  7.02 us

profile of v1, /device:TPU:1, one launch (start us, length us, event | category | flops | bytes accessed | tf_op | source)
XLA Modules:
  0.0 118.8 jit_solution(4148379278295782686)
XLA Ops:
  0.0 34.3 %dispatch.1 = (bf16[16,128,256]{2,1,0:T(8,128)(2,1)}, bf16[4096,128]{1,0:T(8,128)(2,1)}, bf16[4096,128]{1,0:T(8,128)(2,1)}) custom-call(bf16[256,256]{1,0:T(8,128)(2,1)} %q_ref.1, bf16[4096,128]{1,0:T(8,128)(2,1)} %k_ref.3, bf16[4096,128]{1,0:T(8,128)(2,1)} %v_ref.3), custom_call_target="tpu_custom_call" | custom-call | tf_op jit(solution)/shard_map/dispatch/pallas_call | solution.py:141
  34.3 46.7 %attend.1 = (bf16[16,128,256]{2,1,0:T(8,128)(2,1)}, f32[16,8,256]{2,1,0:T(8,128)}) custom-call(s32[8]{0:T(128)} %new_ref.1, s32[8]{0:T(128)} %prior_ref.1, bf16[16,128,256]{2,1,0:T(8,128)(2,1)} %get-tuple-element.10.qg_ref, bf16[4096,128]{1,0:T(8,128)(2,1)} %k_ref.3, bf16[4096,128]{1,0:T(8,128)(2,1)} %v_ref.3, bf16[4096,128]{1,0:T(8,128)(2,1)} %get-tuple-element.11.ko_ref, ...), custom_call_target="tpu_custom_call" | custom-call | tf_op jit(solution)/shard_map/attend/pallas_call | solution.py:293
  81.0 30.8 %combine.1 = bf16[256,2048]{1,0:T(8,128)(2,1)} custom-call(bf16[16,128,256]{2,1,0:T(8,128)(2,1)} %get-tuple-element.13.ot_ref, f32[16,8,256]{2,1,0:T(8,128)} %get-tuple-element.14.st_ref), custom_call_target="tpu_custom_call" | custom-call | tf_op jit(solution)/shard_map/combine/pallas_call | solution.py:390
  111.7 7.0 %convolution_convert_fusion = bf16[256,2048]{1,0:T(8,128)(2,1)} fusion(bf16[256,2048]{1,0:T(8,128)(2,1)} %combine.1, bf16[2048,2048]{1,0:T(8,128)(2,1)} %param.9), kind=kOutput, calls=%fused_computation | convolution fusion | flops 2148007936 | bytes 10485760 | tf_op jit(solution)/shard_map/dot_general | solution.py:416

commit v2 on v1

v2 whole, which is shorter than its diff:
```python
import functools
import math

import jax
import jax.numpy as jnp
from jax import lax
from jax.experimental import pallas as pl
from jax.experimental.pallas import tpu as pltpu
from jax.sharding import PartitionSpec as P

MESH = pl.DeviceIdType.MESH
CTX = 16
HEAD = 8
SIDE = 4
REQS = 8
HALF = 128
WIDTH = 128
HEADS = 2
LANES = HALF * HEADS
KEYS = 4096
PIECE = KEYS // HEAD
CHUNKS = 4
CHUNK = 2 * PIECE // CHUNKS
UNIT = 1024
ALIGN = 128
STEPS = CTX * (2 * KEYS // UNIT) + 4
LOW = -1e9
NEG = -1e30
SCALE = math.log2(math.e) / math.sqrt(WIDTH)
VMEM = 56 * 1024 * 1024


def remote(src, dst, send, recv, ctx, head):
    return pltpu.make_async_remote_copy(
        src_ref=src, dst_ref=dst, send_sem=send, recv_sem=recv, device_id=(ctx, head), device_id_type=MESH
    )


def greet(peers):
    barrier = pltpu.get_barrier_semaphore()
    for ctx, head in peers:
        pl.semaphore_signal(barrier, inc=1, device_id=(ctx, head), device_id_type=MESH)


def meet(peers):
    pl.semaphore_wait(pltpu.get_barrier_semaphore(), len(peers))


def dispatch_kernel(
    q_ref, k_ref, v_ref, qt_ref, kb_ref, vt_ref, qs_ref, vs_ref,
    own_sem, qz_send, qx_send, q_recv, kz_send, ky_send, kc_send, k_recv,
):
    ctx, head = lax.axis_index("ctx"), lax.axis_index("head")
    z, x = ctx // SIDE, ctx % SIDE
    y, core = head // 2, head % 2
    part = ctx // (CTX // 2)
    far = lax.rem(ctx + CTX // 2, CTX)
    twin = y * 2 + (1 - core)

    def zed(d):
        return lax.rem(z + d, SIDE)

    def on_x(d):
        return lax.rem(x + d, SIDE)

    def on_y(d):
        return lax.rem(y + d, SIDE) * 2 + core

    peers = (
        [(zed(d) * SIDE + x, head) for d in (1, 2, 3)]
        + [(z * SIDE + on_x(d), head) for d in (1, 3)]
        + [(ctx, on_y(d)) for d in (1, 3)]
        + [(ctx, twin)]
    )
    greet(peers)
    for rows in range(2):
        for h in range(HEADS):
            block = q_ref[rows * HALF : (rows + 1) * HALF, h * WIDTH : (h + 1) * WIDTH]
            qs_ref[rows, :, h * HALF : (h + 1) * HALF] = block.T

    @pl.loop(0, HEAD)
    def _(p):
        at = pl.multiple_of(p * PIECE, PIECE)
        vs_ref[:, pl.ds(at, PIECE)] = v_ref[pl.ds(at, PIECE), :].T

    meet(peers)
    pending = []

    def start(copy):
        copy.start()
        pending.append(copy)

    def head_offset(p, c):
        return p * PIECE + (c % 2) * CHUNK

    def source(c):
        at = pl.multiple_of(head_offset(head, c), CHUNK)
        return k_ref.at[pl.ds(at, CHUNK), :] if c < 2 else vs_ref.at[:, pl.ds(at, CHUNK)]

    def chunk(side, p, c):
        at = pl.multiple_of(side * KEYS + head_offset(p, c), CHUNK)
        return kb_ref.at[pl.ds(at, CHUNK), :] if c < 2 else vt_ref.at[:, pl.ds(at, CHUNK)]

    def share_q(slot, src, turn, ways):
        for d in ways:
            to = z * SIDE + on_x(d)
            start(remote(src, qt_ref.at[slot], qx_send.at[turn, d - 1], q_recv.at[slot], to, head))

    def arrived_q(slot):
        remote(qt_ref.at[slot], qt_ref.at[slot], qz_send.at[0], q_recv.at[slot], ctx, head).wait_recv()

    def pass_q(d):
        slot = zed(d) * SIDE + x
        arrived_q(slot)
        share_q(slot, qt_ref.at[slot], d, (1, 3))

    def relay_q(d):
        way = 1 if d in (0, 1) else 3
        slot = zed(d) * SIDE + on_x(4 - way)
        arrived_q(slot)
        to = z * SIDE + on_x(way)
        start(remote(qt_ref.at[slot], qt_ref.at[slot], qx_send.at[d, 1], q_recv.at[slot], to, head))

    def arrived_kv(p, c):
        ref = chunk(1 - part, p, c)
        remote(ref, ref, kz_send.at[0], k_recv.at[p, c], ctx, head).wait_recv()

    def send_kv(p, c, sem, to):
        ref = chunk(1 - part, p, c)
        start(remote(ref, ref, sem, k_recv.at[p, c], ctx, to))

    def pass_kv(c):
        arrived_kv(head, c)
        for d in (1, 3):
            send_kv(head, c, ky_send.at[c, d - 1], on_y(d))
        send_kv(head, c, kc_send.at[0, c], twin)

    def relay_kv(c):
        for d in (1, 3):
            p = on_y(d)
            arrived_kv(p, c)
            if (c % 2 == 0) == (d == 3):
                send_kv(p, c, ky_send.at[c, 1], on_y(4 - d))
            send_kv(p, c, kc_send.at[d, c], twin)

    def last_kv(c):
        p = on_y(2)
        arrived_kv(p, c)
        send_kv(p, c, kc_send.at[2, c], twin)

    for c in range(CHUNKS):
        start(remote(source(c), chunk(part, head, c), kz_send.at[c], k_recv.at[head, c], far, head))
        if c == 0:
            for d in (1, 3):
                zt = zed(d)
                start(remote(qs_ref.at[zt // 2], qt_ref.at[ctx], qz_send.at[d - 1], q_recv.at[ctx], zt * SIDE + x, head))
        if c == 1:
            zt = zed(2)
            start(remote(qs_ref.at[zt // 2], qt_ref.at[ctx], qz_send.at[1], q_recv.at[ctx], zt * SIDE + x, head))
    share_q(ctx, qs_ref.at[z // 2], 0, (1, 3))
    own = [
        pltpu.make_async_copy(qs_ref.at[z // 2], qt_ref.at[ctx], own_sem.at[0]),
        pltpu.make_async_copy(k_ref, kb_ref.at[pl.ds(pl.multiple_of(part * KEYS, KEYS), KEYS), :], own_sem.at[1]),
        pltpu.make_async_copy(vs_ref, vt_ref.at[:, pl.ds(pl.multiple_of(part * KEYS, KEYS), KEYS)], own_sem.at[2]),
    ]
    for copy in own:
        copy.start()

    pass_kv(0)
    pass_q(1)
    pass_q(3)
    relay_q(0)
    pass_kv(1)
    pass_q(2)
    relay_kv(0)
    pass_kv(2)
    relay_q(1)
    relay_q(3)
    relay_kv(1)
    pass_kv(3)
    relay_q(2)
    relay_kv(2)
    last_kv(0)
    relay_kv(3)
    last_kv(1)
    last_kv(2)
    last_kv(3)
    for d in range(SIDE):
        row = zed(d) * SIDE
        arrived_q(row + on_x(1 if d in (0, 1) else 3))
        arrived_q(row + on_x(2))
    for c in range(CHUNKS):
        for d in range(SIDE):
            arrived_kv(lax.rem(y + d, SIDE) * 2 + (1 - core), c)
    for copy in own:
        copy.wait()
    for copy in pending:
        copy.wait_send()


def dispatch(queries, keys, values):
    anywhere = pl.BlockSpec(memory_space=pl.ANY)
    vector = pl.BlockSpec(memory_space=pltpu.VMEM)
    dma = pltpu.SemaphoreType.DMA
    return pl.pallas_call(
        dispatch_kernel,
        out_shape=(
            jax.ShapeDtypeStruct((CTX, WIDTH, LANES), queries.dtype),
            jax.ShapeDtypeStruct((2 * KEYS, WIDTH), keys.dtype),
            jax.ShapeDtypeStruct((WIDTH, 2 * KEYS), values.dtype),
        ),
        in_specs=[vector, anywhere, vector],
        out_specs=(anywhere,) * 3,
        scratch_shapes=[
            pltpu.VMEM((2, WIDTH, LANES), queries.dtype),
            pltpu.VMEM((WIDTH, KEYS), values.dtype),
            dma((3,)),
            dma((3,)),
            dma((SIDE, 3)),
            dma((CTX,)),
            dma((CHUNKS,)),
            dma((CHUNKS, 3)),
            dma((SIDE, CHUNKS)),
            dma((HEAD, CHUNKS)),
        ],
        compiler_params=pltpu.CompilerParams(collective_id=0, has_side_effects=True, vmem_limit_bytes=VMEM),
        name="dispatch",
    )(queries, keys, values)


def attend_kernel(where_ref, new_ref, prior_ref, qt_any, k_any, vt_any, ot_ref, st_ref,
                  qt_ref, k_ref, vt_ref, s0_ref, s1_ref, x0_ref, x1_ref, m_ref, l_ref, acc_ref, tile_ref, pos_ref, mask_ref, load_sem):
    loads = [
        pltpu.make_async_copy(src, dst, load_sem.at[i])
        for i, (src, dst) in enumerate(((k_any, k_ref), (qt_any, qt_ref), (vt_any, vt_ref)))
    ]
    for load in loads:
        load.start()
    ctx = where_ref[0]
    half = ctx // (CTX // 2)
    base = lax.rem(ctx, CTX // 2) * KEYS

    q_start, k_start = [jnp.int32(0)], [jnp.int32(0)]
    for r in range(REQS - 1):
        q_start.append(q_start[-1] + new_ref[r])
        k_start.append(k_start[-1] + new_ref[r] + prior_ref[r])
    ahead = [prior_ref[r] + k_start[r] - q_start[r] for r in range(REQS)]
    lower = base
    upper = base + CTX // 2 * KEYS

    def bounds(row):
        lo, hi = jnp.zeros_like(row), jnp.full_like(row, ahead[0])
        for r in range(1, REQS):
            here = row >= q_start[r]
            lo = jnp.where(here, k_start[r], lo)
            hi = jnp.where(here, ahead[r], hi)
        return lo, row + hi

    def span(lo, hi):
        a0 = jnp.clip(lo - lower, 0, KEYS)
        e0 = jnp.clip(hi + 1 - lower, 0, KEYS)
        a1 = jnp.clip(lo - upper, 0, KEYS)
        e1 = jnp.clip(hi + 1 - upper, 0, KEYS)
        return jnp.where(e0 > a0, a0, KEYS + a1), jnp.where(e1 > a1, KEYS + e1, e0)

    def first_row(b):
        return b * (2 * HALF) + half * HALF

    def plan(b, count):
        lo_all, hi_one = bounds(first_row(b))
        lo_one, hi_all = bounds(first_row(b) + HALF - 1)
        begin, end = span(lo_all, hi_all)
        full_begin, full_end = span(lo_one, hi_one)
        full_end = jnp.where(hi_one >= lo_one, full_end, 0)
        begin = begin // ALIGN * ALIGN
        units = jnp.where(end > begin, (end - begin + UNIT - 1) // UNIT, 0)
        begin = jnp.minimum(begin, 2 * KEYS - UNIT * units)

        def put(u, _):
            at = begin + u * UNIT
            tile_ref[count + u] = b
            pos_ref[count + u] = at
            mask_ref[count + u] = jnp.where((at >= full_begin) & (at + UNIT <= full_end), 0, 1)
            return 0

        lax.fori_loop(0, units, put, 0)
        return count + units

    ot_ref[...] = jnp.zeros_like(ot_ref)
    st_ref[...] = jnp.full(st_ref.shape, NEG, jnp.float32)
    acc_ref[...] = jnp.zeros_like(acc_ref)
    l_ref[...] = jnp.zeros_like(l_ref)
    m_ref[...] = jnp.full_like(m_ref, LOW)
    lane = lax.broadcasted_iota(jnp.int32, (1, LANES), 1) % HALF
    count = lax.fori_loop(0, CTX, plan, jnp.int32(0))
    for i in range(3):
        tile_ref[count + i] = jnp.int32(CTX)
        pos_ref[count + i] = jnp.int32(0)
        mask_ref[count + i] = jnp.int32(0)

    def produce(i, s_ref, x_ref, masked):
        b = tile_ref[i]
        at = pl.multiple_of(pos_ref[i], ALIGN)
        s = jnp.dot(k_ref[pl.ds(at, UNIT), :], qt_ref[jnp.minimum(b, CTX - 1)], preferred_element_type=jnp.float32) * SCALE
        if masked:
            begin, end = span(*bounds(first_row(b) + lane))
            key = lax.broadcasted_iota(jnp.int32, (UNIT, LANES), 0)
            s = jnp.where((key >= begin - at) & (key < end - at), s, NEG)
        s_ref[...] = s
        x_ref[...] = jnp.max(s.reshape(UNIT // 8, 8, LANES), axis=0)

    def process(i, s_ref, x_ref):
        b = tile_ref[i]
        at = pl.multiple_of(pos_ref[i], ALIGN)
        first = tile_ref[jnp.maximum(i - 1, 0)] != b
        first = first | (i == 0)
        m_old = jnp.where(first, LOW, m_ref[0:1, :])
        m = jnp.maximum(m_old, jnp.max(x_ref[...], axis=0, keepdims=True))
        alpha = jnp.where(first, 0.0, jnp.exp2(m_old - m))
        p = jnp.exp2(s_ref[...] - m)
        m_ref[...] = jnp.broadcast_to(m, m_ref.shape)
        l_ref[...] = l_ref[...] * alpha + jnp.sum(p.reshape(UNIT // 8, 8, LANES), axis=0)
        acc_ref[...] = acc_ref[...] * alpha + jnp.dot(
            vt_ref[:, pl.ds(at, UNIT)], p.astype(jnp.bfloat16), preferred_element_type=jnp.float32
        )

    def finish(i):
        b = tile_ref[i]

        @pl.when((tile_ref[i + 1] != b) & (b < CTX))
        def _():
            total = jnp.sum(l_ref[...], axis=0, keepdims=True)
            live = total > 0.0
            safe = jnp.where(live, total, 1.0)
            st_ref[b] = jnp.broadcast_to(jnp.where(live, m_ref[0:1, :] + jnp.log2(safe), NEG), (8, LANES))
            ot_ref[b] = (acc_ref[...] * (1.0 / safe)).astype(ot_ref.dtype)

    def step(i, now, later):
        masked = mask_ref[i + 1] == 1

        @pl.when(masked)
        def _():
            produce(i + 1, *later, True)
            process(i, *now)

        @pl.when(jnp.logical_not(masked))
        def _():
            produce(i + 1, *later, False)
            process(i, *now)

        finish(i)

    even, odd = (s0_ref, x0_ref), (s1_ref, x1_ref)
    for load in loads:
        load.wait()
    produce(0, *even, True)

    @pl.loop(0, (count + 1) // 2)
    def _(i):
        step(2 * i, even, odd)
        step(2 * i + 1, odd, even)


def attend(where, new_counts, prior_lengths, gathered, keys, turned):
    scalars = pl.BlockSpec(memory_space=pltpu.SMEM)
    vector = pl.BlockSpec(memory_space=pltpu.VMEM)
    return pl.pallas_call(
        attend_kernel,
        out_shape=(
            jax.ShapeDtypeStruct((CTX, WIDTH, LANES), jnp.bfloat16),
            jax.ShapeDtypeStruct((CTX, 8, LANES), jnp.float32),
        ),
        in_specs=[scalars] * 3 + [pl.BlockSpec(memory_space=pl.ANY)] * 3,
        out_specs=(vector, vector),
        scratch_shapes=[
            pltpu.VMEM(gathered.shape, gathered.dtype),
            pltpu.VMEM(keys.shape, keys.dtype),
            pltpu.VMEM(turned.shape, turned.dtype),
            pltpu.VMEM((UNIT, LANES), jnp.float32),
            pltpu.VMEM((UNIT, LANES), jnp.float32),
            pltpu.VMEM((8, LANES), jnp.float32),
            pltpu.VMEM((8, LANES), jnp.float32),
            pltpu.VMEM((8, LANES), jnp.float32),
            pltpu.VMEM((8, LANES), jnp.float32),
            pltpu.VMEM((WIDTH, LANES), jnp.float32),
            pltpu.SMEM((STEPS,), jnp.int32),
            pltpu.SMEM((STEPS,), jnp.int32),
            pltpu.SMEM((STEPS,), jnp.int32),
            pltpu.SemaphoreType.DMA((3,)),
        ],
        compiler_params=pltpu.CompilerParams(vmem_limit_bytes=VMEM),
        name="attend",
    )(where, new_counts, prior_lengths, gathered, keys, turned)


def combine_kernel(
    ot_ref, st_ref, att_ref, og_ref, sg_ref, own_sem, o_send, s_send, o_recv, s_recv, y_send, c_send, a_recv
):
    ctx, head = lax.axis_index("ctx"), lax.axis_index("head")
    y, core = head // 2, head % 2
    twin = y * 2 + (1 - core)

    def on_y(d):
        return lax.rem(y + d, SIDE) * 2 + core

    peers = (
        [(lax.rem(ctx + d, CTX), head) for d in range(1, CTX)]
        + [(ctx, on_y(d)) for d in (1, 2, 3)]
        + [(ctx, twin)]
    )
    greet(peers)
    meet(peers)
    pending = []

    def start(copy):
        copy.start()
        pending.append(copy)

    for d in range(1, CTX):
        to = lax.rem(ctx + d, CTX)
        start(remote(st_ref.at[to], sg_ref.at[ctx], s_send.at[d], s_recv.at[ctx], to, head))
        start(remote(ot_ref.at[to], og_ref.at[ctx], o_send.at[d], o_recv.at[ctx], to, head))
    own = [
        pltpu.make_async_copy(ot_ref.at[ctx], og_ref.at[ctx], own_sem.at[0]),
        pltpu.make_async_copy(st_ref.at[ctx], sg_ref.at[ctx], own_sem.at[1]),
    ]
    for copy in own:
        copy.start()
    for copy in own:
        copy.wait()
    for d in range(1, CTX):
        of = lax.rem(ctx + d, CTX)
        remote(sg_ref.at[of], sg_ref.at[of], s_send.at[0], s_recv.at[of], ctx, head).wait_recv()
        remote(og_ref.at[of], og_ref.at[of], o_send.at[0], o_recv.at[of], ctx, head).wait_recv()

    def slot(p):
        return att_ref.at[:, pl.ds(pl.multiple_of(p * LANES, LANES), LANES)]

    mine = slot(head)
    for half in range(2):
        members = range(half * CTX // 2, (half + 1) * CTX // 2)
        top = sg_ref[members[0], 0:1, :]
        for i in members[1:]:
            top = jnp.maximum(top, sg_ref[i, 0:1, :])
        shares = [jnp.exp2(sg_ref[i, 0:1, :] - top) for i in members]
        inverse = 1.0 / functools.reduce(jnp.add, shares)
        out = jnp.zeros((WIDTH, LANES), jnp.float32)
        for i, share in zip(members, shares):
            out += og_ref[i].astype(jnp.float32) * (share * inverse)
        for h in range(HEADS):
            mine[half * HALF : (half + 1) * HALF, h * WIDTH : (h + 1) * WIDTH] = (
                out[:, h * HALF : (h + 1) * HALF].T.astype(att_ref.dtype)
            )

    for d in (1, 3, 2):
        start(remote(mine, mine, y_send.at[d - 1], a_recv.at[head], ctx, on_y(d)))
    start(remote(mine, mine, c_send.at[0], a_recv.at[head], ctx, twin))

    def arrived(p):
        remote(slot(p), slot(p), c_send.at[0], a_recv.at[p], ctx, head).wait_recv()

    for d in (1, 3, 2):
        p = on_y(d)
        arrived(p)
        start(remote(slot(p), slot(p), c_send.at[d], a_recv.at[p], ctx, twin))
    for d in range(SIDE):
        arrived(lax.rem(y + d, SIDE) * 2 + (1 - core))
    for copy in pending:
        copy.wait_send()


def combine(outs, logs):
    anywhere = pl.BlockSpec(memory_space=pl.ANY)
    dma = pltpu.SemaphoreType.DMA
    return pl.pallas_call(
        combine_kernel,
        out_shape=jax.ShapeDtypeStruct((2 * HALF, HEAD * LANES), outs.dtype),
        in_specs=[anywhere] * 2,
        out_specs=pl.BlockSpec(memory_space=pltpu.VMEM),
        scratch_shapes=[
            pltpu.VMEM(outs.shape, outs.dtype),
            pltpu.VMEM(logs.shape, logs.dtype),
            dma((2,)),
            dma((CTX,)),
            dma((CTX,)),
            dma((CTX,)),
            dma((CTX,)),
            dma((3,)),
            dma((SIDE,)),
            dma((HEAD,)),
        ],
        compiler_params=pltpu.CompilerParams(collective_id=1, has_side_effects=True, vmem_limit_bytes=VMEM),
        name="combine",
    )(outs, logs)


def body(queries, keys, values, w_out, new_counts, prior_lengths):
    where = lax.axis_index("ctx").astype(jnp.int32).reshape(1)
    gathered, cache, turned = dispatch(queries, keys, values)
    outs, logs = attend(where, new_counts, prior_lengths, gathered, cache, turned)
    attended = combine(outs, logs)
    return jnp.dot(attended, w_out, preferred_element_type=jnp.float32).astype(jnp.bfloat16)


def solution(mesh):
    return jax.shard_map(
        body,
        mesh=mesh,
        in_specs=(P("ctx", "head"), P("ctx", None), P("ctx", None), P(None, "head"), P(), P()),
        out_specs=P("ctx", "head"),
        check_vma=False,
    )
```

time: 119 us -> 104 us (0.87)
  the two profiles are of different devices: /device:TPU:1 before, /device:TPU:7 now
where the time goes in v2:
time: 104 us; the launch traced here: 102 us
  Pallas kernels  94.7 us (91%)
  matrix products  7.02 us (7%)
    pallas_call x1, Pallas kernels, dispatch(): pl.pallas_call(dispatch_kernel, out_shape=(jax.ShapeDtypeStruct((CTX, WID...  38.9 us
    pallas_call x1, Pallas kernels, combine(): pl.pallas_call(combine_kernel, out_shape=jax.ShapeDtypeStruct((2 * HALF,...  35.6 us
    pallas_call x1, Pallas kernels, attend(): pl.pallas_call(attend_kernel, out_shape=(jax.ShapeDtypeStruct((CTX, WIDTH...  20.2 us
    dot_general x1, matrix products, body(): jnp.dot(attended, w_out, preferred_element_type=jnp.float32)  7.02 us

profile of v2, /device:TPU:7, one launch (start us, length us, event | category | flops | bytes accessed | tf_op | source)
XLA Modules:
  0.0 101.7 jit_solution(6907224282239033583)
XLA Ops:
  0.0 38.9 %dispatch.1 = (bf16[16,128,256]{2,1,0:T(8,128)(2,1)}, bf16[8192,128]{1,0:T(8,128)(2,1)}, bf16[128,8192]{1,0:T(8,128)(2,1)}) custom-call(bf16[256,256]{1,0:T(8,128)(2,1)} %q_ref.1, bf16[4096,128]{1,0:T(8,128)(2,1)} %k_ref.1, bf16[4096,128]{1,0:T(8,128)(2,1)} %v_ref.1), custom_call_target="tpu_custom_call" | custom-call | tf_op jit(solution)/shard_map/dispatch/pallas_call | solution.py:205
  38.9 20.2 %attend.1 = (bf16[16,128,256]{2,1,0:T(8,128)(2,1)}, f32[16,8,256]{2,1,0:T(8,128)}) custom-call(s32[1]{0:T(128)} %bitcast.where_ref, s32[8]{0:T(128)} %new_ref.1, s32[8]{0:T(128)} %prior_ref.1, bf16[16,128,256]{2,1,0:T(8,128)(2,1)} %get-tuple-element.10.qt_any, bf16[8192,128]{1,0:T(8,128)(2,1)} %get-tuple-element.11.k_any, ...), custom_call_target="tpu_custom_call" | custom-call | tf_op jit(solution)/shard_map/attend/pallas_call | solution.py:367
  59.1 35.6 %combine.1 = bf16[256,2048]{1,0:T(8,128)(2,1)} custom-call(bf16[16,128,256]{2,1,0:T(8,128)(2,1)} %get-tuple-element.13.ot_ref, f32[16,8,256]{2,1,0:T(8,128)} %get-tuple-element.14.st_ref), custom_call_target="tpu_custom_call" | custom-call | tf_op jit(solution)/shard_map/combine/pallas_call | solution.py:475
  94.7 7.0 %convolution_convert_fusion = bf16[256,2048]{1,0:T(8,128)(2,1)} fusion(bf16[256,2048]{1,0:T(8,128)(2,1)} %combine.1, bf16[2048,2048]{1,0:T(8,128)(2,1)} %param.9), kind=kOutput, calls=%fused_computation | convolution fusion | flops 2148007936 | bytes 10485760 | tf_op jit(solution)/shard_map/dot_general | solution.py:502

commit v3 on v2

v3 whole, which is shorter than its diff:
```python
import functools
import math

import jax
import jax.numpy as jnp
from jax import lax
from jax.experimental import pallas as pl
from jax.experimental.pallas import tpu as pltpu
from jax.sharding import PartitionSpec as P

MESH = pl.DeviceIdType.MESH
CTX = 16
HEAD = 8
SIDE = 4
REQS = 8
HALF = 128
WIDTH = 128
HEADS = 2
LANES = HALF * HEADS
KEYS = 4096
PIECE = KEYS // HEAD
CHUNKS = 4
CHUNK = 2 * PIECE // CHUNKS
COLUMNS = 512
FAR_FIRST = (
    (2, 2), (2, 1), (1, 2), (2, 3), (3, 2), (1, 1), (3, 3), (1, 3), (3, 1), (2, 0), (0, 2), (0, 1), (1, 0), (0, 3), (3, 0)
)
UNIT = 1024
ALIGN = CHUNK
STEPS = CTX * (2 * KEYS // UNIT) + 4
LOW = -1e9
NEG = -1e30
SCALE = math.log2(math.e) / math.sqrt(WIDTH)
VMEM = 56 * 1024 * 1024


def remote(src, dst, send, recv, ctx, head):
    return pltpu.make_async_remote_copy(
        src_ref=src, dst_ref=dst, send_sem=send, recv_sem=recv, device_id=(ctx, head), device_id_type=MESH
    )


def greet(peers):
    barrier = pltpu.get_barrier_semaphore()
    for ctx, head in peers:
        pl.semaphore_signal(barrier, inc=1, device_id=(ctx, head), device_id_type=MESH)


def meet(peers):
    pl.semaphore_wait(pltpu.get_barrier_semaphore(), len(peers))


def dispatch_kernel(
    q_ref, k_ref, v_ref, qt_ref, kf_ref, vf_ref, vo_ref, qs_ref, vs_ref,
    own_sem, qz_send, qx_send, q_recv, kz_send, ky_send, kc_send, k_recv,
):
    ctx, head = lax.axis_index("ctx"), lax.axis_index("head")
    z, x = ctx // SIDE, ctx % SIDE
    y, core = head // 2, head % 2
    far = lax.rem(ctx + CTX // 2, CTX)
    twin = y * 2 + (1 - core)

    def zed(d):
        return lax.rem(z + d, SIDE)

    def on_x(d):
        return lax.rem(x + d, SIDE)

    def on_y(d):
        return lax.rem(y + d, SIDE) * 2 + core

    peers = (
        [(zed(d) * SIDE + x, head) for d in (1, 2, 3)]
        + [(z * SIDE + on_x(d), head) for d in (1, 2, 3)]
        + [(ctx, on_y(d)) for d in (1, 2, 3)]
        + [(ctx, twin)]
    )
    greet(peers)
    for rows in range(2):
        for h in range(HEADS):
            block = q_ref[rows * HALF : (rows + 1) * HALF, h * WIDTH : (h + 1) * WIDTH]
            qs_ref[rows, :, h * HALF : (h + 1) * HALF] = block.T

    @pl.loop(0, KEYS // CHUNK)
    def _(p):
        vs_ref[p] = v_ref[pl.ds(pl.multiple_of(p * CHUNK, CHUNK), CHUNK), :].T

    meet(peers)
    pending = []

    def start(copy):
        copy.start()
        pending.append(copy)

    def number(p, c):
        return p * (PIECE // CHUNK) + c % 2

    def source(c):
        i = number(head, c)
        return k_ref.at[pl.ds(pl.multiple_of(i * CHUNK, CHUNK), CHUNK), :] if c < 2 else vs_ref.at[i]

    def chunk(p, c):
        i = number(p, c)
        return kf_ref.at[pl.ds(pl.multiple_of(i * CHUNK, CHUNK), CHUNK), :] if c < 2 else vf_ref.at[i]

    def share_q(slot, src, turn, ways):
        for d in ways:
            to = z * SIDE + on_x(d)
            start(remote(src, qt_ref.at[slot], qx_send.at[turn, d - 1], q_recv.at[slot], to, head))

    def arrived_q(slot):
        remote(qt_ref.at[slot], qt_ref.at[slot], qz_send.at[0], q_recv.at[slot], ctx, head).wait_recv()

    def pass_q(d):
        slot = zed(d) * SIDE + x
        arrived_q(slot)
        share_q(slot, qt_ref.at[slot], d, (1, 3, 2))

    def arrived_kv(p, c):
        ref = chunk(p, c)
        remote(ref, ref, kz_send.at[0], k_recv.at[p, c], ctx, head).wait_recv()

    def send_kv(p, c, sem, to):
        ref = chunk(p, c)
        start(remote(ref, ref, sem, k_recv.at[p, c], ctx, to))

    def pass_kv(c):
        arrived_kv(head, c)
        for d in (1, 3, 2):
            send_kv(head, c, ky_send.at[c, d - 1], on_y(d))
        send_kv(head, c, kc_send.at[0, c], twin)

    def relay_kv(c):
        for d in (1, 3):
            p = on_y(d)
            arrived_kv(p, c)
            send_kv(p, c, kc_send.at[d, c], twin)

    def last_kv(c):
        p = on_y(2)
        arrived_kv(p, c)
        send_kv(p, c, kc_send.at[2, c], twin)

    for c in range(CHUNKS):
        start(remote(source(c), chunk(head, c), kz_send.at[c], k_recv.at[head, c], far, head))
        if c == 0:
            for d in (1, 3):
                zt = zed(d)
                start(remote(qs_ref.at[zt // 2], qt_ref.at[ctx], qz_send.at[d - 1], q_recv.at[ctx], zt * SIDE + x, head))
        if c == 1:
            zt = zed(2)
            start(remote(qs_ref.at[zt // 2], qt_ref.at[ctx], qz_send.at[1], q_recv.at[ctx], zt * SIDE + x, head))
    share_q(ctx, qs_ref.at[z // 2], 0, (1, 3, 2))
    own = [
        pltpu.make_async_copy(qs_ref.at[z // 2], qt_ref.at[ctx], own_sem.at[0]),
        pltpu.make_async_copy(vs_ref, vo_ref, own_sem.at[1]),
    ]
    for copy in own:
        copy.start()

    pass_kv(0)
    pass_q(1)
    pass_q(3)
    pass_kv(1)
    pass_q(2)
    relay_kv(0)
    pass_kv(2)
    relay_kv(1)
    pass_kv(3)
    relay_kv(2)
    last_kv(0)
    relay_kv(3)
    last_kv(1)
    last_kv(2)
    last_kv(3)
    for d in range(SIDE):
        row = zed(d) * SIDE
        arrived_q(row + on_x(1))
        arrived_q(row + on_x(3))
        arrived_q(row + on_x(2))
    for c in range(CHUNKS):
        for d in range(SIDE):
            arrived_kv(lax.rem(y + d, SIDE) * 2 + (1 - core), c)
    for copy in own:
        copy.wait()
    for copy in pending:
        copy.wait_send()


def dispatch(queries, keys, values):
    anywhere = pl.BlockSpec(memory_space=pl.ANY)
    vector = pl.BlockSpec(memory_space=pltpu.VMEM)
    dma = pltpu.SemaphoreType.DMA
    return pl.pallas_call(
        dispatch_kernel,
        out_shape=(
            jax.ShapeDtypeStruct((CTX, WIDTH, LANES), queries.dtype),
            jax.ShapeDtypeStruct((KEYS, WIDTH), keys.dtype),
            jax.ShapeDtypeStruct((KEYS // CHUNK, WIDTH, CHUNK), values.dtype),
            jax.ShapeDtypeStruct((KEYS // CHUNK, WIDTH, CHUNK), values.dtype),
        ),
        in_specs=[vector, anywhere, vector],
        out_specs=(anywhere,) * 4,
        scratch_shapes=[
            pltpu.VMEM((2, WIDTH, LANES), queries.dtype),
            pltpu.VMEM((KEYS // CHUNK, WIDTH, CHUNK), values.dtype),
            dma((2,)),
            dma((3,)),
            dma((SIDE, 3)),
            dma((CTX,)),
            dma((CHUNKS,)),
            dma((CHUNKS, 3)),
            dma((SIDE, CHUNKS)),
            dma((HEAD, CHUNKS)),
        ],
        compiler_params=pltpu.CompilerParams(collective_id=0, has_side_effects=True, vmem_limit_bytes=VMEM),
        name="dispatch",
    )(queries, keys, values)


def attend_kernel(where_ref, new_ref, prior_ref, qt_any, k_any, kf_any, vo_any, vf_any, ot_ref, st_ref,
                  qt_ref, k_ref, vt_ref, s0_ref, s1_ref, x0_ref, x1_ref, m_ref, l_ref, acc_ref, tile_ref, pos_ref, mask_ref, load_sem):
    ctx = where_ref[0]
    half = ctx // (CTX // 2)
    mine, other = pl.multiple_of(half * KEYS, KEYS), pl.multiple_of((1 - half) * KEYS, KEYS)
    blocks = KEYS // CHUNK
    loads = [
        pltpu.make_async_copy(src, dst, load_sem.at[i])
        for i, (src, dst) in enumerate(
            (
                (qt_any, qt_ref),
                (k_any, k_ref.at[pl.ds(mine, KEYS), :]),
                (kf_any, k_ref.at[pl.ds(other, KEYS), :]),
                (vo_any, vt_ref.at[pl.ds(half * blocks, blocks)]),
                (vf_any, vt_ref.at[pl.ds((1 - half) * blocks, blocks)]),
            )
        )
    ]
    for load in loads:
        load.start()
    base = lax.rem(ctx, CTX // 2) * KEYS

    q_start, k_start = [jnp.int32(0)], [jnp.int32(0)]
    for r in range(REQS - 1):
        q_start.append(q_start[-1] + new_ref[r])
        k_start.append(k_start[-1] + new_ref[r] + prior_ref[r])
    ahead = [prior_ref[r] + k_start[r] - q_start[r] for r in range(REQS)]
    lower = base
    upper = base + CTX // 2 * KEYS

    def bounds(row):
        lo, hi = jnp.zeros_like(row), jnp.full_like(row, ahead[0])
        for r in range(1, REQS):
            here = row >= q_start[r]
            lo = jnp.where(here, k_start[r], lo)
            hi = jnp.where(here, ahead[r], hi)
        return lo, row + hi

    def span(lo, hi):
        a0 = jnp.clip(lo - lower, 0, KEYS)
        e0 = jnp.clip(hi + 1 - lower, 0, KEYS)
        a1 = jnp.clip(lo - upper, 0, KEYS)
        e1 = jnp.clip(hi + 1 - upper, 0, KEYS)
        return jnp.where(e0 > a0, a0, KEYS + a1), jnp.where(e1 > a1, KEYS + e1, e0)

    def first_row(b):
        return b * (2 * HALF) + half * HALF

    def plan(b, count):
        lo_all, hi_one = bounds(first_row(b))
        lo_one, hi_all = bounds(first_row(b) + HALF - 1)
        begin, end = span(lo_all, hi_all)
        full_begin, full_end = span(lo_one, hi_one)
        full_end = jnp.where(hi_one >= lo_one, full_end, 0)
        begin = begin // ALIGN * ALIGN
        units = jnp.where(end > begin, (end - begin + UNIT - 1) // UNIT, 0)
        begin = jnp.minimum(begin, 2 * KEYS - UNIT * units)

        def put(u, _):
            at = begin + u * UNIT
            tile_ref[count + u] = b
            pos_ref[count + u] = at
            mask_ref[count + u] = jnp.where((at >= full_begin) & (at + UNIT <= full_end), 0, 1)
            return 0

        lax.fori_loop(0, units, put, 0)
        return count + units

    ot_ref[...] = jnp.zeros_like(ot_ref)
    st_ref[...] = jnp.full(st_ref.shape, NEG, jnp.float32)
    acc_ref[...] = jnp.zeros_like(acc_ref)
    l_ref[...] = jnp.zeros_like(l_ref)
    m_ref[...] = jnp.full_like(m_ref, LOW)
    lane = lax.broadcasted_iota(jnp.int32, (1, LANES), 1) % HALF
    count = lax.fori_loop(0, CTX, plan, jnp.int32(0))
    for i in range(3):
        tile_ref[count + i] = jnp.int32(CTX)
        pos_ref[count + i] = jnp.int32(0)
        mask_ref[count + i] = jnp.int32(0)

    def produce(i, s_ref, x_ref, masked):
        b = tile_ref[i]
        at = pl.multiple_of(pos_ref[i], ALIGN)
        s = jnp.dot(k_ref[pl.ds(at, UNIT), :], qt_ref[jnp.minimum(b, CTX - 1)], preferred_element_type=jnp.float32) * SCALE
        if masked:
            begin, end = span(*bounds(first_row(b) + lane))
            key = lax.broadcasted_iota(jnp.int32, (UNIT, LANES), 0)
            s = jnp.where((key >= begin - at) & (key < end - at), s, NEG)
        s_ref[...] = s
        x_ref[...] = jnp.max(s.reshape(UNIT // 8, 8, LANES), axis=0)

    def process(i, s_ref, x_ref):
        b = tile_ref[i]
        at = pl.multiple_of(pos_ref[i], ALIGN)
        first = tile_ref[jnp.maximum(i - 1, 0)] != b
        first = first | (i == 0)
        m_old = jnp.where(first, LOW, m_ref[0:1, :])
        m = jnp.maximum(m_old, jnp.max(x_ref[...], axis=0, keepdims=True))
        alpha = jnp.where(first, 0.0, jnp.exp2(m_old - m))
        p = jnp.exp2(s_ref[...] - m)
        m_ref[...] = jnp.broadcast_to(m, m_ref.shape)
        l_ref[...] = l_ref[...] * alpha + jnp.sum(p.reshape(UNIT // 8, 8, LANES), axis=0)
        p = p.astype(jnp.bfloat16)
        total = acc_ref[...] * alpha
        for j in range(UNIT // CHUNK):
            total += jnp.dot(
                vt_ref[at // CHUNK + j], p[j * CHUNK : (j + 1) * CHUNK], preferred_element_type=jnp.float32
            )
        acc_ref[...] = total

    def finish(i):
        b = tile_ref[i]

        @pl.when((tile_ref[i + 1] != b) & (b < CTX))
        def _():
            total = jnp.sum(l_ref[...], axis=0, keepdims=True)
            live = total > 0.0
            safe = jnp.where(live, total, 1.0)
            log = jnp.where(live, m_ref[0:1, :] + jnp.log2(safe), NEG)
            out = (acc_ref[...] * (1.0 / safe)).astype(ot_ref.dtype)
            for h in range(HEADS):
                st_ref[b, h : h + 1, :] = log[:, h * HALF : (h + 1) * HALF]
                ot_ref[b, h] = out[:, h * HALF : (h + 1) * HALF]

    def step(i, now, later):
        masked = mask_ref[i + 1] == 1

        @pl.when(masked)
        def _():
            produce(i + 1, *later, True)
            process(i, *now)

        @pl.when(jnp.logical_not(masked))
        def _():
            produce(i + 1, *later, False)
            process(i, *now)

        finish(i)

    even, odd = (s0_ref, x0_ref), (s1_ref, x1_ref)
    for load in loads:
        load.wait()
    produce(0, *even, True)

    @pl.loop(0, (count + 1) // 2)
    def _(i):
        step(2 * i, even, odd)
        step(2 * i + 1, odd, even)


def attend(where, new_counts, prior_lengths, gathered, keys, far_keys, turned, far_turned):
    scalars = pl.BlockSpec(memory_space=pltpu.SMEM)
    vector = pl.BlockSpec(memory_space=pltpu.VMEM)
    return pl.pallas_call(
        attend_kernel,
        out_shape=(
            jax.ShapeDtypeStruct((CTX, HEADS, WIDTH, HALF), jnp.bfloat16),
            jax.ShapeDtypeStruct((CTX, 8, HALF), jnp.float32),
        ),
        in_specs=[scalars] * 3 + [pl.BlockSpec(memory_space=pl.ANY)] * 5,
        out_specs=(vector, vector),
        scratch_shapes=[
            pltpu.VMEM(gathered.shape, gathered.dtype),
            pltpu.VMEM((2 * KEYS, WIDTH), keys.dtype),
            pltpu.VMEM((2 * KEYS // CHUNK, WIDTH, CHUNK), turned.dtype),
            pltpu.VMEM((UNIT, LANES), jnp.float32),
            pltpu.VMEM((UNIT, LANES), jnp.float32),
            pltpu.VMEM((8, LANES), jnp.float32),
            pltpu.VMEM((8, LANES), jnp.float32),
            pltpu.VMEM((8, LANES), jnp.float32),
            pltpu.VMEM((8, LANES), jnp.float32),
            pltpu.VMEM((WIDTH, LANES), jnp.float32),
            pltpu.SMEM((STEPS,), jnp.int32),
            pltpu.SMEM((STEPS,), jnp.int32),
            pltpu.SMEM((STEPS,), jnp.int32),
            pltpu.SemaphoreType.DMA((5,)),
        ],
        compiler_params=pltpu.CompilerParams(vmem_limit_bytes=VMEM),
        name="attend",
    )(where, new_counts, prior_lengths, gathered, keys, far_keys, turned, far_turned)


def finish_kernel(
    ot_ref, st_ref, w_any, out_ref, og_ref, sg_ref, att_ref, w_ref, acc_ref,
    w_sem, own_sem, o_send, s_send, o_recv, s_recv, y_send, c_send, a_recv,
):
    ctx, head = lax.axis_index("ctx"), lax.axis_index("head")
    z, x = ctx // SIDE, ctx % SIDE
    y, core = head // 2, head % 2
    twin = y * 2 + (1 - core)

    def on_y(d):
        return lax.rem(y + d, SIDE) * 2 + core

    def at(steps):
        return lax.rem(z + steps[0], SIDE) * SIDE + lax.rem(x + steps[1], SIDE)

    peers = [(at(steps), head) for steps in FAR_FIRST] + [(ctx, on_y(d)) for d in (1, 2, 3)] + [(ctx, twin)]
    greet(peers)
    weights = pltpu.make_async_copy(w_any, w_ref, w_sem)
    weights.start()
    own = [pltpu.make_async_copy(st_ref.at[ctx], sg_ref.at[ctx], own_sem.at[0])]
    own += [pltpu.make_async_copy(ot_ref.at[ctx, h], og_ref.at[h, ctx], own_sem.at[1 + h]) for h in range(HEADS)]
    for copy in own:
        copy.start()
    meet(peers)
    pending = []

    def start(copy):
        copy.start()
        pending.append(copy)

    for i, steps in enumerate(FAR_FIRST):
        to = at(steps)
        start(remote(st_ref.at[to], sg_ref.at[ctx], s_send.at[i], s_recv.at[ctx], to, head))
        start(remote(ot_ref.at[to, 0], og_ref.at[0, ctx], o_send.at[0, i], o_recv.at[0, ctx], to, head))
    for h in range(1, HEADS):
        for i, steps in enumerate(FAR_FIRST):
            to = at(steps)
            start(remote(ot_ref.at[to, h], og_ref.at[h, ctx], o_send.at[h, i], o_recv.at[h, ctx], to, head))
    for copy in own:
        copy.wait()
    for steps in FAR_FIRST:
        of = at(steps)
        remote(sg_ref.at[of], sg_ref.at[of], s_send.at[0], s_recv.at[of], ctx, head).wait_recv()

    def arrived(h, p):
        ref = att_ref.at[h, p]
        remote(ref, ref, c_send.at[h, 0], a_recv.at[h, p], ctx, head).wait_recv()

    for h in range(HEADS):
        for steps in FAR_FIRST:
            of = at(steps)
            ref = og_ref.at[h, of]
            remote(ref, ref, o_send.at[h, 0], o_recv.at[h, of], ctx, head).wait_recv()
        for half in range(2):
            members = range(half * CTX // 2, (half + 1) * CTX // 2)
            logs = [sg_ref[i, h : h + 1, :] for i in members]
            top = functools.reduce(jnp.maximum, logs)
            shares = [jnp.exp2(log - top) for log in logs]
            inverse = 1.0 / functools.reduce(jnp.add, shares)
            out = jnp.zeros((WIDTH, HALF), jnp.float32)
            for i, share in zip(members, shares):
                out += og_ref[h, i].astype(jnp.float32) * (share * inverse)
            att_ref[h, head, half * HALF : (half + 1) * HALF, :] = out.T.astype(att_ref.dtype)
        mine = att_ref.at[h, head]
        for d in (2, 1, 3):
            start(remote(mine, mine, y_send.at[h, d - 1], a_recv.at[h, head], ctx, on_y(d)))
        start(remote(mine, mine, c_send.at[h, 0], a_recv.at[h, head], ctx, twin))
        for d in (1, 3, 2):
            p = on_y(d)
            arrived(h, p)
            ref = att_ref.at[h, p]
            start(remote(ref, ref, c_send.at[h, d], a_recv.at[h, p], ctx, twin))
        for d in range(SIDE):
            arrived(h, lax.rem(y + d, SIDE) * 2 + (1 - core))
        if h == 0:
            weights.wait()
        left = jnp.concatenate([att_ref[h, p] for p in range(HEAD)], axis=1)

        @pl.loop(0, w_ref.shape[2] // COLUMNS)
        def _(n):
            columns = pl.ds(pl.multiple_of(n * COLUMNS, COLUMNS), COLUMNS)
            right = jnp.concatenate([w_ref[HEADS * p + h, :, columns] for p in range(HEAD)], axis=0)
            product = jnp.dot(left, right, preferred_element_type=jnp.float32)
            if h == 0:
                acc_ref[:, columns] = product
            else:
                out_ref[:, columns] = (acc_ref[:, columns] + product).astype(out_ref.dtype)

    for copy in pending:
        copy.wait_send()


def finish(outs, logs, w_out):
    anywhere = pl.BlockSpec(memory_space=pl.ANY)
    dma = pltpu.SemaphoreType.DMA
    rows, width = 2 * HALF, w_out.shape[1]
    blocks = w_out.reshape(HEAD * HEADS, WIDTH, width)
    return pl.pallas_call(
        finish_kernel,
        out_shape=jax.ShapeDtypeStruct((rows, width), outs.dtype),
        in_specs=[anywhere] * 3,
        out_specs=pl.BlockSpec(memory_space=pltpu.VMEM),
        scratch_shapes=[
            pltpu.VMEM((HEADS, CTX, WIDTH, HALF), outs.dtype),
            pltpu.VMEM(logs.shape, logs.dtype),
            pltpu.VMEM((HEADS, HEAD, rows, WIDTH), outs.dtype),
            pltpu.VMEM(blocks.shape, blocks.dtype),
            pltpu.VMEM((rows, width), jnp.float32),
            dma,
            dma((1 + HEADS,)),
            dma((HEADS, CTX)),
            dma((CTX,)),
            dma((HEADS, CTX)),
            dma((CTX,)),
            dma((HEADS, 3)),
            dma((HEADS, SIDE)),
            dma((HEADS, HEAD)),
        ],
        compiler_params=pltpu.CompilerParams(collective_id=1, has_side_effects=True, vmem_limit_bytes=VMEM),
        name="finish",
    )(outs, logs, blocks)


def body(queries, keys, values, w_out, new_counts, prior_lengths):
    where = lax.axis_index("ctx").astype(jnp.int32).reshape(1)
    gathered, far_keys, far_turned, turned = dispatch(queries, keys, values)
    outs, logs = attend(where, new_counts, prior_lengths, gathered, keys, far_keys, turned, far_turned)
    return finish(outs, logs, w_out)


def solution(mesh):
    return jax.shard_map(
        body,
        mesh=mesh,
        in_specs=(P("ctx", "head"), P("ctx", None), P("ctx", None), P(None, "head"), P(), P()),
        out_specs=P("ctx", "head"),
        check_vma=False,
    )
```

time: 104 us -> 91.3 us (0.88); the launches traced: 102 us -> 91.1 us
  matrix products: 7.02 us -> 0 us
  Pallas kernels: 94.7 us -> 88.7 us
  local copies, waits for them, and re-layouts: 0 us -> 2.3 us
    pallas_call x1, Pallas kernels: 38.9 us -> 27.6 us  [dispatch(): pl.pallas_call(dispatch_kernel, out_shape=(jax.ShapeDtypeStruct((CTX, WID...]
    dot_general x1 -> x0, matrix products: 7.02 us -> none  [body(): jnp.dot(attended, w_out, preferred_element_type=jnp.float32)]
    pallas_call x2, Pallas kernels: 55.8 us -> 61.1 us  [the longest x1 38.9 us: finish(): pl.pallas_call(finish_kernel, out_shape=jax.ShapeDtypeStruct((rows, width...]
    unnamed x0 -> x1, local copies, waits for them, and re-layouts: none -> 2.3 us
where the time goes in v3:
time: 91.3 us; the launch traced here: 91.1 us
  Pallas kernels  88.7 us (97%)
  local copies, waits for them, and re-layouts  2.3 us (3%)
    pallas_call x1, Pallas kernels, finish(): pl.pallas_call(finish_kernel, out_shape=jax.ShapeDtypeStruct((rows, width...  38.9 us
    pallas_call x1, Pallas kernels, dispatch(): pl.pallas_call(dispatch_kernel, out_shape=(jax.ShapeDtypeStruct((CTX, WID...  27.6 us
    pallas_call x1, Pallas kernels, attend(): pl.pallas_call(attend_kernel, out_shape=(jax.ShapeDtypeStruct((CTX, HEADS...  22.2 us
    unnamed x1, local copies, waits for them, and re-layouts  2.3 us

profile of v3, /device:TPU:7, one launch (start us, length us, event | category | flops | bytes accessed | tf_op | source)
XLA Modules:
  0.0 91.1 jit_solution(2620586612180413437)
XLA Ops:
  0.0 27.6 %dispatch.1 = (bf16[16,128,256]{2,1,0:T(8,128)(2,1)}, bf16[4096,128]{1,0:T(8,128)(2,1)}, bf16[16,128,256]{2,1,0:T(8,128)(2,1)}, bf16[16,128,256]{2,1,0:T(8,128)(2,1)}) custom-call(bf16[256,256]{1,0:T(8,128)(2,1)} %q_ref.1, bf16[4096,128]{1,0:T(8,128)(2,1)} %k_any.1, bf16[4096,128]{1,0:T(8,128)(2,1)} %v_ref.1), custom_call_target="tpu_custom_call" | custom-call | tf_op jit(solution)/shard_map/dispatch/pallas_call | solution.py:194
  27.6 22.2 %attend.1 = (bf16[16,2,128,128]{3,2,1,0:T(8,128)(2,1)}, f32[16,8,128]{2,1,0:T(8,128)}) custom-call(s32[1]{0:T(128)} %bitcast.where_ref, s32[8]{0:T(128)} %new_ref.1, s32[8]{0:T(128)} %prior_ref.1, bf16[16,128,256]{2,1,0:T(8,128)(2,1)} %get-tuple-element.11.qt_any, bf16[4096,128]{1,0:T(8,128)(2,1)} %k_any.1, bf16[4096,128]{1,0:T(8,128)(2,1)} %get-tuple-element.12.kf_any, ...), custom_call_target="tpu_custom_call" | custom-call | tf_op jit(solution)/shard_map/attend/pallas_call | solution.py:374
  49.8 38.9 %finish.1 = bf16[256,2048]{1,0:T(8,128)(2,1)} custom-call(bf16[16,2,128,128]{3,2,1,0:T(8,128)(2,1)} %get-tuple-element.15.ot_ref, f32[16,8,128]{2,1,0:T(8,128)} %get-tuple-element.16.st_ref, bf16[16,128,2048]{2,1,0:T(8,128)(2,1)} %bitcast.2), custom_call_target="tpu_custom_call" | custom-call | tf_op jit(solution)/shard_map/finish/pallas_call | solution.py:500
  88.8 2.3 %copy.8 = bf16[256,2048]{1,0:T(8,128)(2,1)} copy(bf16[256,2048]{1,0:T(8,128)(2,1)} %finish.1) | data formatting | bytes 2097152

commit v4 on v3

--- a/solution.py
+++ b/solution.py
@@ -25,9 +25,10 @@
 FAR_FIRST = (
     (2, 2), (2, 1), (1, 2), (2, 3), (3, 2), (1, 1), (3, 3), (1, 3), (3, 1), (2, 0), (0, 2), (0, 1), (1, 0), (0, 3), (3, 0)
 )
-UNIT = 1024
+UNIT = 2048
+PART = 1024
 ALIGN = CHUNK
-STEPS = CTX * (2 * KEYS // UNIT) + 4
+STEPS = CTX * (2 * KEYS // PART + 1) + 4
 LOW = -1e9
 NEG = -1e30
 SCALE = math.log2(math.e) / math.sqrt(WIDTH)
@@ -51,7 +52,7 @@
 
 
 def dispatch_kernel(
-    q_ref, k_ref, v_ref, qt_ref, kf_ref, vf_ref, vo_ref, qs_ref, vs_ref,
+    q_any, k_ref, v_any, qt_ref, kf_ref, vf_ref, vo_ref, q_ref, v_ref, qs_ref, vs_ref,
     own_sem, qz_send, qx_send, q_recv, kz_send, ky_send, kc_send, k_recv,
 ):
     ctx, head = lax.axis_index("ctx"), lax.axis_index("head")
@@ -76,10 +77,19 @@
         + [(ctx, twin)]
     )
     greet(peers)
+    loads = [
+        pltpu.make_async_copy(q_any, q_ref, own_sem.at[0]),
+        pltpu.make_async_copy(v_any, v_ref, own_sem.at[1]),
+    ]
+    for load in loads:
+        load.start()
+    loads[0].wait()
     for rows in range(2):
         for h in range(HEADS):
             block = q_ref[rows * HALF : (rows + 1) * HALF, h * WIDTH : (h + 1) * WIDTH]
             qs_ref[rows, :, h * HALF : (h + 1) * HALF] = block.T
+
+    loads[1].wait()
 
     @pl.loop(0, KEYS // CHUNK)
     def _(p):
@@ -189,7 +199,7 @@
 
 def dispatch(queries, keys, values):
     anywhere = pl.BlockSpec(memory_space=pl.ANY)
-    vector = pl.BlockSpec(memory_space=pltpu.VMEM)
+    held = pl.BlockSpec(memory_space=pltpu.HBM)
     dma = pltpu.SemaphoreType.DMA
     return pl.pallas_call(
         dispatch_kernel,
@@ -199,9 +209,11 @@
             jax.ShapeDtypeStruct((KEYS // CHUNK, WIDTH, CHUNK), values.dtype),
             jax.ShapeDtypeStruct((KEYS // CHUNK, WIDTH, CHUNK), values.dtype),
         ),
-        in_specs=[vector, anywhere, vector],
+        in_specs=[held] * 3,
         out_specs=(anywhere,) * 4,
         scratch_shapes=[
+            pltpu.VMEM(queries.shape, queries.dtype),
+            pltpu.VMEM(values.shape, values.dtype),
             pltpu.VMEM((2, WIDTH, LANES), queries.dtype),
             pltpu.VMEM((KEYS // CHUNK, WIDTH, CHUNK), values.dtype),
             dma((2,)),
@@ -213,13 +225,13 @@
             dma((SIDE, CHUNKS)),
             dma((HEAD, CHUNKS)),
         ],
-        compiler_params=pltpu.CompilerParams(collective_id=0, has_side_effects=True, vmem_limit_bytes=VMEM),
+        compiler_params=pltpu.CompilerParams(collective_id=0, has_side_effects=True, vmem_limit_bytes=48 * 1024 * 1024),
         name="dispatch",
     )(queries, keys, values)
 
 
 def attend_kernel(where_ref, new_ref, prior_ref, qt_any, k_any, kf_any, vo_any, vf_any, ot_ref, st_ref,
-                  qt_ref, k_ref, vt_ref, s0_ref, s1_ref, x0_ref, x1_ref, m_ref, l_ref, acc_ref, tile_ref, pos_ref, mask_ref, load_sem):
+                  qt_ref, k_ref, vt_ref, s0_ref, s1_ref, x0_ref, x1_ref, m_ref, l_ref, acc_ref, tile_ref, pos_ref, part_ref, load_sem):
     ctx = where_ref[0]
     half = ctx // (CTX // 2)
     mine, other = pl.multiple_of(half * KEYS, KEYS), pl.multiple_of((1 - half) * KEYS, KEYS)
@@ -272,23 +284,21 @@
         begin, end = span(lo_all, hi_all)
         full_begin, full_end = span(lo_one, hi_one)
         full_end = jnp.where(hi_one >= lo_one, full_end, 0)
-        begin = begin // ALIGN * ALIGN
-        units = jnp.where(end > begin, (end - begin + UNIT - 1) // UNIT, 0)
-        begin = jnp.minimum(begin, 2 * KEYS - UNIT * units)
-
-        def put(u, _):
-            at = begin + u * UNIT
-            tile_ref[count + u] = b
-            pos_ref[count + u] = at
-            mask_ref[count + u] = jnp.where((at >= full_begin) & (at + UNIT <= full_end), 0, 1)
-            return 0
-
-        lax.fori_loop(0, units, put, 0)
-        return count + units
+
+        def put(state):
+            at, i = state
+            full = (at >= full_begin) & (at + UNIT <= full_end)
+            tile_ref[i] = b
+            pos_ref[i] = at
+            part_ref[i] = jnp.where(full, 0, 1)
+            return at + jnp.where(full, UNIT, PART), i + 1
+
+        return lax.while_loop(lambda state: state[0] < end, put, (begin // ALIGN * ALIGN, count))[1]
 
     ot_ref[...] = jnp.zeros_like(ot_ref)
     st_ref[...] = jnp.full(st_ref.shape, NEG, jnp.float32)
     acc_ref[...] = jnp.zeros_like(acc_ref)
+    vt_ref[2 * blocks :] = jnp.zeros((PART // CHUNK, WIDTH, CHUNK), vt_ref.dtype)
     l_ref[...] = jnp.zeros_like(l_ref)
     m_ref[...] = jnp.full_like(m_ref, LOW)
     lane = lax.broadcasted_iota(jnp.int32, (1, LANES), 1) % HALF
@@ -296,20 +306,22 @@
     for i in range(3):
         tile_ref[count + i] = jnp.int32(CTX)
         pos_ref[count + i] = jnp.int32(0)
-        mask_ref[count + i] = jnp.int32(0)
-
-    def produce(i, s_ref, x_ref, masked):
+        part_ref[count + i] = jnp.int32(1)
+
+    def produce(i, s_ref, x_ref, part):
+        size = PART if part else UNIT
         b = tile_ref[i]
         at = pl.multiple_of(pos_ref[i], ALIGN)
-        s = jnp.dot(k_ref[pl.ds(at, UNIT), :], qt_ref[jnp.minimum(b, CTX - 1)], preferred_element_type=jnp.float32) * SCALE
-        if masked:
+        s = jnp.dot(k_ref[pl.ds(at, size), :], qt_ref[jnp.minimum(b, CTX - 1)], preferred_element_type=jnp.float32) * SCALE
+        if part:
             begin, end = span(*bounds(first_row(b) + lane))
-            key = lax.broadcasted_iota(jnp.int32, (UNIT, LANES), 0)
+            key = lax.broadcasted_iota(jnp.int32, (size, LANES), 0)
             s = jnp.where((key >= begin - at) & (key < end - at), s, NEG)
-        s_ref[...] = s
-        x_ref[...] = jnp.max(s.reshape(UNIT // 8, 8, LANES), axis=0)
-
-    def process(i, s_ref, x_ref):
+        s_ref[:size, :] = s
+        x_ref[...] = jnp.max(s.reshape(size // 8, 8, LANES), axis=0)
+
+    def process(i, s_ref, x_ref, part):
+        size = PART if part else UNIT
         b = tile_ref[i]
         at = pl.multiple_of(pos_ref[i], ALIGN)
         first = tile_ref[jnp.maximum(i - 1, 0)] != b
@@ -317,12 +329,12 @@
         m_old = jnp.where(first, LOW, m_ref[0:1, :])
         m = jnp.maximum(m_old, jnp.max(x_ref[...], axis=0, keepdims=True))
         alpha = jnp.where(first, 0.0, jnp.exp2(m_old - m))
-        p = jnp.exp2(s_ref[...] - m)
+        p = jnp.exp2(s_ref[:size, :] - m)
         m_ref[...] = jnp.broadcast_to(m, m_ref.shape)
-        l_ref[...] = l_ref[...] * alpha + jnp.sum(p.reshape(UNIT // 8, 8, LANES), axis=0)
+        l_ref[...] = l_ref[...] * alpha + jnp.sum(p.reshape(size // 8, 8, LANES), axis=0)
         p = p.astype(jnp.bfloat16)
         total = acc_ref[...] * alpha
-        for j in range(UNIT // CHUNK):
+        for j in range(size // CHUNK):
             total += jnp.dot(
                 vt_ref[at // CHUNK + j], p[j * CHUNK : (j + 1) * CHUNK], preferred_element_type=jnp.float32
             )
@@ -343,24 +355,24 @@
                 ot_ref[b, h] = out[:, h * HALF : (h + 1) * HALF]
 
     def step(i, now, later):
-        masked = mask_ref[i + 1] == 1
-
-        @pl.when(masked)
-        def _():
-            produce(i + 1, *later, True)
-            process(i, *now)
-
-        @pl.when(jnp.logical_not(masked))
-        def _():
-            produce(i + 1, *later, False)
-            process(i, *now)
+        for after in range(2):
+            for before in range(2):
+
+                @pl.when((part_ref[i + 1] == after) & (part_ref[i] == before))
+                def _():
+                    produce(i + 1, *later, after)
+                    process(i, *now, before)
 
         finish(i)
 
     even, odd = (s0_ref, x0_ref), (s1_ref, x1_ref)
     for load in loads:
         load.wait()
-    produce(0, *even, True)
+    for after in range(2):
+
+        @pl.when(part_ref[0] == after)
+        def _():
+            produce(0, *even, after)
 
     @pl.loop(0, (count + 1) // 2)
     def _(i):
@@ -377,12 +389,12 @@
             jax.ShapeDtypeStruct((CTX, HEADS, WIDTH, HALF), jnp.bfloat16),
             jax.ShapeDtypeStruct((CTX, 8, HALF), jnp.float32),
         ),
-        in_specs=[scalars] * 3 + [pl.BlockSpec(memory_space=pl.ANY)] * 5,
+        in_specs=[scalars] * 3 + [pl.BlockSpec(memory_space=pl.ANY), pl.BlockSpec(memory_space=pltpu.HBM)] + [pl.BlockSpec(memory_space=pl.ANY)] * 3,
         out_specs=(vector, vector),
         scratch_shapes=[
             pltpu.VMEM(gathered.shape, gathered.dtype),
-            pltpu.VMEM((2 * KEYS, WIDTH), keys.dtype),
-            pltpu.VMEM((2 * KEYS // CHUNK, WIDTH, CHUNK), turned.dtype),
+            pltpu.VMEM((2 * KEYS + PART, WIDTH), keys.dtype),
+            pltpu.VMEM(((2 * KEYS + PART) // CHUNK, WIDTH, CHUNK), turned.dtype),
             pltpu.VMEM((UNIT, LANES), jnp.float32),
             pltpu.VMEM((UNIT, LANES), jnp.float32),
             pltpu.VMEM((8, LANES), jnp.float32),
@@ -395,7 +407,7 @@
             pltpu.SMEM((STEPS,), jnp.int32),
             pltpu.SemaphoreType.DMA((5,)),
         ],
-        compiler_params=pltpu.CompilerParams(vmem_limit_bytes=VMEM),
+        compiler_params=pltpu.CompilerParams(vmem_limit_bytes=48 * 1024 * 1024),
         name="attend",
     )(where, new_counts, prior_lengths, gathered, keys, far_keys, turned, far_turned)
 
@@ -496,11 +508,11 @@
     anywhere = pl.BlockSpec(memory_space=pl.ANY)
     dma = pltpu.SemaphoreType.DMA
     rows, width = 2 * HALF, w_out.shape[1]
-    blocks = w_out.reshape(HEAD * HEADS, WIDTH, width)
+    blocks = pltpu.with_memory_space_constraint(w_out.reshape(HEAD * HEADS, WIDTH, width), pltpu.HBM)
     return pl.pallas_call(
         finish_kernel,
         out_shape=jax.ShapeDtypeStruct((rows, width), outs.dtype),
-        in_specs=[anywhere] * 3,
+        in_specs=[anywhere, anywhere, pl.BlockSpec(memory_space=pltpu.HBM)],
         out_specs=pl.BlockSpec(memory_space=pltpu.VMEM),
         scratch_shapes=[
             pltpu.VMEM((HEADS, CTX, WIDTH, HALF), outs.dtype),
@@ -518,12 +530,15 @@
             dma((HEADS, SIDE)),
             dma((HEADS, HEAD)),
         ],
-        compiler_params=pltpu.CompilerParams(collective_id=1, has_side_effects=True, vmem_limit_bytes=VMEM),
+        compiler_params=pltpu.CompilerParams(collective_id=1, has_side_effects=True, vmem_limit_bytes=48 * 1024 * 1024),
         name="finish",
     )(outs, logs, blocks)
 
 
-def body(queries, keys, values, w_out, new_counts, prior_lengths):
+def body(*operands):
+    w_out = operands[3]
+    held = [pltpu.with_memory_space_constraint(array, pltpu.HBM) for array in operands if array is not w_out]
+    queries, keys, values, new_counts, prior_lengths = held
     where = lax.axis_index("ctx").astype(jnp.int32).reshape(1)
     gathered, far_keys, far_turned, turned = dispatch(queries, keys, values)
     outs, logs = attend(where, new_counts, prior_lengths, gathered, keys, far_keys, turned, far_turned)

time: 91.3 us -> 80.8 us (0.88)
  Pallas kernels: 88.7 us -> 79.7 us
  local copies, waits for them, and re-layouts: 2.3 us -> 0.97 us
    pallas_call x1, Pallas kernels: 38.9 us -> 34.4 us  [finish(): pl.pallas_call(finish_kernel, out_shape=jax.ShapeDtypeStruct((rows, width...]
    pallas_call x1, Pallas kernels: 22.2 us -> 18.9 us  [attend(): pl.pallas_call(attend_kernel, out_shape=(jax.ShapeDtypeStruct((CTX, HEADS...]
    unnamed x1, local copies, waits for them, and re-layouts: 2.3 us -> 0.97 us
    pallas_call x1, Pallas kernels: 27.6 us -> 26.4 us  [dispatch(): pl.pallas_call(dispatch_kernel, out_shape=(jax.ShapeDtypeStruct((CTX, WID...]
where the time goes in v4:
time: 80.8 us; the launch traced here: 80.7 us
  Pallas kernels  79.7 us (99%)
  local copies, waits for them, and re-layouts  0.97 us (1%)
    pallas_call x1, Pallas kernels, finish(): pl.pallas_call(finish_kernel, out_shape=jax.ShapeDtypeStruct((rows, width...  34.4 us
    pallas_call x1, Pallas kernels, dispatch(): pl.pallas_call(dispatch_kernel, out_shape=(jax.ShapeDtypeStruct((CTX, WID...  26.4 us
    pallas_call x1, Pallas kernels, attend(): pl.pallas_call(attend_kernel, out_shape=(jax.ShapeDtypeStruct((CTX, HEADS...  18.9 us

profile of v4, /device:TPU:7, one launch (start us, length us, event | category | flops | bytes accessed | tf_op | source)
XLA Modules:
  0.0 80.7 jit_solution(16964291186864752789)
XLA Ops:
  0.0 26.4 %dispatch.1 = (bf16[16,128,256]{2,1,0:T(8,128)(2,1)S(1)}, bf16[4096,128]{1,0:T(8,128)(2,1)S(1)}, bf16[16,128,256]{2,1,0:T(8,128)(2,1)S(1)}, bf16[16,128,256]{2,1,0:T(8,128)(2,1)S(1)}) custom-call(bf16[256,256]{1,0:T(8,128)(2,1)} %q_any.1, bf16[4096,128]{1,0:T(8,128)(2,1)} %k_any.1, bf16[4096,128]{1,0:T(8,128)(2,1)} %v_any.1), custom_call_target="tpu_custom_call" | custom-call | tf_op jit(solution)/shard_map/dispatch/pallas_call | solution.py:204
  26.4 18.9 %attend.1 = (bf16[16,2,128,128]{3,2,1,0:T(8,128)(2,1)S(1)}, f32[16,8,128]{2,1,0:T(8,128)S(1)}) custom-call(s32[1]{0:T(128)} %bitcast.where_ref, s32[8]{0:T(128)} %new_ref.1, s32[8]{0:T(128)} %prior_ref.1, bf16[16,128,256]{2,1,0:T(8,128)(2,1)S(1)} %get-tuple-element.11.qt_any, bf16[4096,128]{1,0:T(8,128)(2,1)} %k_any.1, ...), custom_call_target="tpu_custom_call" | custom-call | tf_op jit(solution)/shard_map/attend/pallas_call | solution.py:386
  45.3 34.4 %finish.1 = bf16[256,2048]{1,0:T(8,128)(2,1)S(1)} custom-call(bf16[16,2,128,128]{3,2,1,0:T(8,128)(2,1)S(1)} %get-tuple-element.15.ot_ref, f32[16,8,128]{2,1,0:T(8,128)S(1)} %get-tuple-element.16.st_ref, bf16[16,128,2048]{2,1,0:T(8,128)(2,1)} %bitcast.2), custom_call_target="tpu_custom_call" | custom-call | tf_op jit(solution)/shard_map/finish/pallas_call | solution.py:512
  79.7 1.0 %copy.8 = bf16[256,2048]{1,0:T(8,128)(2,1)} copy(bf16[256,2048]{1,0:T(8,128)(2,1)S(1)} %finish.1) | data formatting | bytes 2097152
